TPU v7x, 128 devices: a whole 4x4x4 slice. The times are simulated.
128 devices in a mesh: dp: 16 (over x, y_lo, core), tensor: 8 (over y_hi, z).
Axes of the slice: x: 4, y: 4 (y_hi: 2, y_lo: 2; y = y_hi * 2 + y_lo), z: 4, core: 2. Of those that a mesh axis runs over, the one named last changes fastest.
Arguments:
- tokens: bfloat16 [24576, 1536], P(('dp', 'tensor')), may hold values from -6 to 6
- seq_lens: int32 [16, 4], P('dp'), may hold values from 0 to 1536, as said below
- query_key_value_weight: bfloat16 [1536, 3072], P(None, 'tensor'), may hold values from -0.15625 to 0.15625
- out_weight: bfloat16 [1536, 1536], P('tensor'), may hold values from -1 to 1
- gate_up_weight: bfloat16 [2, 1536, 4096], P(None, None, 'tensor'), may hold values from -0.15625 to 0.15625
- down_weight: bfloat16 [4096, 1536], P('tensor'), may hold values from -0.09375 to 0.09375
- norm_gains: float32 [2, 1536], replicated, may hold values from 0.5 to 1.5
- cotangent: bfloat16 [24576, 1536], P(('dp', 'tensor')), may hold values from -6 to 6
Outputs:
- mixed: bfloat16 [24576, 1536], P(('dp', 'tensor'))
- input_grad: float32 [24576, 1536], P(('dp', 'tensor'))
- qkv_grad: float32 [1536, 3072], P('dp', 'tensor')
- out_grad: float32 [1536, 1536], P('tensor', 'dp')
- gate_up_grad: float32 [2, 1536, 4096], P(None, 'dp', 'tensor')
- down_grad: float32 [4096, 1536], P('tensor', 'dp')
- gains_grad: float32 [2, 1536], P(None, 'dp')
Inputs may be any that keep to these rules, and one draw needn't show every extreme that they name: `seq_lens`: row g lists the lengths of the sequences of data group g in slot order; each starts where the one before ends, rounded up to a multiple of 128 tokens, and all end within 1536 tokens; a zero is an empty slot. In every row the first or the second sequence begins within the group's first 192 token slots and ends within its last 192; in some row the first has exactly 1536 tokens.
All inputs are finite; a program needn't handle non-finite values.
Results may differ from a plain program's by a relative error of at most 0.028.
Values may be sent and summed in bfloat16 or wider, within the bound.
A program may use at most 192 MiB of HBM per device.

v0:
```python
import jax
import jax.numpy as jnp
from jax import lax
from jax.sharding import Mesh
from jax.sharding import PartitionSpec as P

HEAD_SIZE = 96
BLOCK = 128
DP = ("dp_0", "dp_1", "dp_2")
DP_TENSOR = ("dp_0", "dp_1", "dp_2", "tensor")


EPSILON = 1e-05
THETA = 100000.0
masked_score = -1e30


def split_up(value, dim, size):
    before, after = (value.shape[:dim], value.shape[dim + 1 :])
    return jnp.moveaxis(value.reshape(*before, size, -1, *after), dim, 0)


def sent_and_summed(value, axis, dim):
    tiles = split_up(value, dim, lax.axis_size(axis))
    arrived = lax.all_to_all(tiles, axis, split_axis=0, concat_axis=0, tiled=True)
    return arrived.astype(jnp.float32).sum(axis=0)


def summed_rows(value, axes, dim):
    far, near = axes
    tiles = split_up(value, dim, lax.axis_size(far))
    nearer = sent_and_summed(tiles, near, dim + 1)
    arrived = lax.all_to_all(
        nearer.astype(jnp.bfloat16), far, split_axis=0, concat_axis=0, tiled=True
    )
    return arrived.astype(jnp.float32).sum(axis=0)


def side_by_side(arrays, axis, dim, along):
    widths = [a.shape[along] for a in arrays]
    both = jnp.concatenate(arrays, axis=along)
    out = summed_rows(both, axis, dim)
    return tuple(jnp.split(out, [sum(widths[:k]) for k in range(1, len(widths))], axis=along))


def sent_to_all(value, axis):
    copies = jnp.broadcast_to(value, (lax.axis_size(axis), *value.shape))
    return lax.all_to_all(copies, axis, split_axis=0, concat_axis=0, tiled=True)


def taken_together(value, axis):
    everything = sent_to_all(value, axis)
    return jnp.sum(everything, axis=0)


def layout(lengths, total_rows):
    padded_rows = (lengths + BLOCK - 1) // BLOCK * BLOCK
    starts = jnp.cumsum(padded_rows, dtype=jnp.int32) - padded_rows
    places = jnp.arange(total_rows, dtype=jnp.int32)[:, None]
    inside = (places >= starts[None, :]) & (places < (starts + lengths)[None, :])
    slot_ids = jnp.arange(lengths.shape[0], dtype=jnp.int32)
    segment = jnp.sum(jnp.where(inside, slot_ids[None, :], 0), axis=1, dtype=jnp.int32)
    offset = jnp.sum(jnp.where(inside, starts[None, :], 0), axis=1, dtype=jnp.int32)
    anywhere = jnp.any(inside, axis=1)
    positions = places[:, 0] - offset
    segment = jnp.where(anywhere, segment, lengths.shape[0] + places[:, 0])
    return (segment, positions)


def angles(positions):
    exponent = jnp.arange(0, HEAD_SIZE, 2, dtype=jnp.float32) / HEAD_SIZE
    inverse = jnp.power(THETA, -exponent)
    phases = positions.astype(jnp.float32)[:, None] * inverse[None, :]
    return (jnp.cos(phases), jnp.sin(phases))


def rotate(values, cos_part, sin_part):
    half_width = values.shape[-1] // 2
    first_half = values[..., :half_width]
    second_half = values[..., half_width:]
    return jnp.concatenate(
        [
            first_half * cos_part - second_half * sin_part,
            second_half * cos_part + first_half * sin_part,
        ],
        axis=-1,
    )


def unrotate(values, cos_part, sin_part):
    half_width = values.shape[-1] // 2
    first_half = values[..., :half_width]
    second_half = values[..., half_width:]
    return jnp.concatenate(
        [
            first_half * cos_part + second_half * sin_part,
            second_half * cos_part - first_half * sin_part,
        ],
        axis=-1,
    )


def times_transposed(left, right):
    return lax.dot_general(
        left, right, (((1,), (1,)), ((), ())), preferred_element_type=jnp.float32
    )


def transposed_times(left, right):
    return lax.dot_general(
        left, right, (((0,), (0,)), ((), ())), preferred_element_type=jnp.float32
    )


def normalize(values):
    scale = lax.rsqrt(jnp.mean(values * values, axis=-1, keepdims=True) + EPSILON)
    return (values * scale, scale)


def norm_back(grad_out, normalized, scale, gain_row):
    scaled = grad_out * gain_row
    through = scale * (scaled - normalized * jnp.mean(scaled * normalized, axis=-1, keepdims=True))
    return (through, jnp.sum(grad_out * normalized, axis=0))


def per_device(
    tokens,
    seq_lens,
    query_key_value_weight,
    out_weight,
    gate_up_weight,
    down_weight,
    norm_gains,
    cotangent,
):
    shard_rows = tokens.shape[0]
    group_rows = shard_rows * lax.axis_size("tensor")
    kv_local = query_key_value_weight.shape[1] // (4 * HEAD_SIZE)
    block_rows = min(512, group_rows)
    block_count = group_rows // block_rows
    scaling = HEAD_SIZE ** (-0.5)
    hidden = tokens.astype(jnp.float32)
    unit_one, scale_one = normalize(hidden)
    normed = (unit_one * norm_gains[0]).astype(jnp.bfloat16)
    normed_all = lax.all_gather(normed, "tensor", axis=0, tiled=True)
    projected_rows = jnp.dot(normed_all, query_key_value_weight, preferred_element_type=jnp.float32)
    projected_rows = projected_rows.reshape(group_rows, kv_local, 4, HEAD_SIZE)
    segment, positions = layout(seq_lens[0], group_rows)
    cos_part, sin_part = angles(positions)
    queries = rotate(
        projected_rows[:, :, 0:2], cos_part[:, None, None], sin_part[:, None, None]
    ).astype(jnp.bfloat16)
    keys_all = rotate(projected_rows[:, :, 2], cos_part[:, None], sin_part[:, None]).astype(
        jnp.bfloat16
    )
    values_all = projected_rows[:, :, 3].astype(jnp.bfloat16)

    def block_scores(first_row):
        query_block = queries[first_row : first_row + block_rows]
        scores = (
            jnp.einsum("qhjd,khd->hjqk", query_block, keys_all, preferred_element_type=jnp.float32)
            * scaling
        )
        block_segment = segment[first_row : first_row + block_rows]
        block_positions = positions[first_row : first_row + block_rows]
        allowed = (block_segment[:, None] == segment[None, :]) & (
            positions[None, :] <= block_positions[:, None]
        )
        return (query_block, jnp.where(allowed[None, None], scores, masked_score))

    attended_list = []
    log_sums = []
    for block_index in range(block_count):
        scores = block_scores(block_index * block_rows)[1]
        row_peak = jnp.max(scores, axis=-1, keepdims=True)
        numerators = jnp.exp(scores - row_peak)
        totals = jnp.sum(numerators, axis=-1, keepdims=True)
        softmax_weights = (numerators / totals).astype(jnp.bfloat16)
        log_sums.append(row_peak + jnp.log(totals))
        attended = jnp.einsum(
            "hjqk,khd->qhjd", softmax_weights, values_all, preferred_element_type=jnp.float32
        )
        attended_list.append(attended.reshape(block_rows, kv_local * 2 * HEAD_SIZE))
    mixed_heads = jnp.concatenate(attended_list, axis=0).astype(jnp.bfloat16)
    branch = lax.psum_scatter(
        jnp.dot(mixed_heads, out_weight, preferred_element_type=jnp.float32).astype(jnp.bfloat16),
        "tensor",
        scatter_dimension=0,
        tiled=True,
    ).astype(jnp.float32)
    middle = hidden + branch
    unit_two, scale_two = normalize(middle)
    normed_two = (unit_two * norm_gains[1]).astype(jnp.bfloat16)
    normed_two_all = lax.all_gather(normed_two, "tensor", axis=0, tiled=True)
    gate_up = jnp.einsum(
        "td,cdf->ctf", normed_two_all, gate_up_weight, preferred_element_type=jnp.float32
    )
    sigmoid_gate = jax.nn.sigmoid(gate_up[0])
    silu_gate = gate_up[0] * sigmoid_gate
    activated = (silu_gate * gate_up[1]).astype(jnp.bfloat16)
    ffn_out = lax.psum_scatter(
        jnp.dot(activated, down_weight, preferred_element_type=jnp.float32).astype(jnp.bfloat16),
        "tensor",
        scatter_dimension=0,
        tiled=True,
    ).astype(jnp.float32)
    mixed = (middle + ffn_out).astype(jnp.bfloat16)
    upstream = cotangent.astype(jnp.float32)
    upstream_all = lax.all_gather(cotangent, "tensor", axis=0, tiled=True)
    grad_act = times_transposed(upstream_all, down_weight)
    down_grad = transposed_times(activated, upstream_all)
    grad_gate = grad_act * gate_up[1] * sigmoid_gate * (1.0 + gate_up[0] * (1.0 - sigmoid_gate))
    grad_upper = grad_act * silu_gate
    grad_gate_up = jnp.stack([grad_gate, grad_upper]).astype(jnp.bfloat16)
    gate_up_grad = jnp.einsum(
        "td,ctf->cdf", normed_two_all, grad_gate_up, preferred_element_type=jnp.float32
    )
    normed_two_part = jnp.einsum(
        "ctf,cdf->td", grad_gate_up, gate_up_weight, preferred_element_type=jnp.float32
    )
    grad_normed_two = lax.psum_scatter(
        normed_two_part.astype(jnp.bfloat16), "tensor", scatter_dimension=0, tiled=True
    ).astype(jnp.float32)
    through_two, gain_two_part = norm_back(grad_normed_two, unit_two, scale_two, norm_gains[1])
    grad_middle = upstream + through_two
    grad_branch_all = lax.all_gather(grad_middle.astype(jnp.bfloat16), "tensor", axis=0, tiled=True)
    grad_heads = times_transposed(grad_branch_all, out_weight).astype(jnp.bfloat16)
    out_grad = transposed_times(mixed_heads, grad_branch_all)
    grad_heads = grad_heads.reshape(group_rows, kv_local, 2, HEAD_SIZE)
    key_grad = jnp.zeros((group_rows, kv_local, HEAD_SIZE), jnp.float32)
    value_grad = jnp.zeros((group_rows, kv_local, HEAD_SIZE), jnp.float32)
    query_grads = []
    for block_index in range(block_count):
        first_row = block_index * block_rows
        query_block, scores = block_scores(first_row)
        softmax_weights = jnp.exp(scores - log_sums[block_index])
        soft_low = softmax_weights.astype(jnp.bfloat16)
        grad_block = grad_heads[first_row : first_row + block_rows]
        grad_weights = jnp.einsum(
            "qhjd,khd->hjqk", grad_block, values_all, preferred_element_type=jnp.float32
        )
        centered = jnp.sum(softmax_weights * grad_weights, axis=-1, keepdims=True)
        grad_scores = (softmax_weights * (grad_weights - centered)).astype(jnp.bfloat16)
        query_grads.append(
            jnp.einsum("hjqk,khd->qhjd", grad_scores, keys_all, preferred_element_type=jnp.float32)
            * scaling
        )
        key_grad = (
            key_grad
            + jnp.einsum(
                "hjqk,qhjd->khd", grad_scores, query_block, preferred_element_type=jnp.float32
            )
            * scaling
        )
        value_grad = value_grad + jnp.einsum(
            "hjqk,qhjd->khd", soft_low, grad_block, preferred_element_type=jnp.float32
        )
    query_grad = unrotate(
        jnp.concatenate(query_grads, axis=0), cos_part[:, None, None], sin_part[:, None, None]
    )
    key_grad = unrotate(key_grad, cos_part[:, None], sin_part[:, None])
    grad_projected = jnp.concatenate(
        [query_grad, key_grad[:, :, None], value_grad[:, :, None]], axis=2
    )
    grad_projected = grad_projected.reshape(group_rows, kv_local * 4 * HEAD_SIZE).astype(
        jnp.bfloat16
    )
    qkv_grad = transposed_times(normed_all, grad_projected)
    normed_part = times_transposed(grad_projected, query_key_value_weight)
    grad_normed = lax.psum_scatter(
        normed_part.astype(jnp.bfloat16), "tensor", scatter_dimension=0, tiled=True
    ).astype(jnp.float32)
    through_one, gain_one_part = norm_back(grad_normed, unit_one, scale_one, norm_gains[0])
    input_grad = grad_middle + through_one
    reduced = (
        summed_rows(qkv_grad.astype(jnp.bfloat16), (("dp_0", "dp_1"), "dp_2"), 0),
        summed_rows(out_grad.astype(jnp.bfloat16), (("dp_0", "dp_1"), "dp_2"), 1),
        summed_rows(gate_up_grad.astype(jnp.bfloat16), (("dp_0", "dp_1"), "dp_2"), 1),
        *side_by_side(
            (
                down_grad.astype(jnp.bfloat16),
                jnp.stack([gain_one_part, gain_two_part]).astype(jnp.bfloat16),
            ),
            (("dp_0", "dp_1"), "dp_2"),
            1,
            0,
        ),
    )
    gains_grad = taken_together(reduced[4], "tensor")
    return (mixed, input_grad, reduced[0], reduced[1], reduced[2], reduced[3], gains_grad)


def solution(mesh):
    split = Mesh(
        mesh.devices.reshape(4, 2, 2, mesh.shape["tensor"]), ("dp_0", "dp_1", "dp_2", "tensor")
    )
    placed = (
        P(DP_TENSOR, None),
        P(DP, None),
        P(None, "tensor"),
        P("tensor", None),
        P(None, None, "tensor"),
        P("tensor", None),
        P(),
        P(DP_TENSOR, None),
    )
    return jax.shard_map(
        per_device,
        mesh=split,
        in_specs=placed,
        out_specs=(
            P(DP_TENSOR, None),
            P(DP_TENSOR, None),
            P(DP, "tensor"),
            P("tensor", DP),
            P(None, DP, "tensor"),
            P("tensor", DP),
            P(None, DP),
        ),
        check_vma=False,
    )
```

profile of v0, /device:TPU:1, one launch (start us, length us, event | category | flops | bytes accessed | tf_op | source)
XLA Modules:
  0.0 813.7 jit_solution(4628204512146934735)
XLA Ops:
  10.1 2.1 fusion.93
  14.0 1.9 multiply_cosine_fusion
  16.0 3.3 compare_and_fusion.2
  19.3 71.8 %all-gather.5.cloned.1.call-done = bf16[1536,1536]{1,0:T(8,128)(2,1)} async-done(((bf16[192,1536]{1,0:T(8,128)(2,1)}), bf16[1536,1536]{1,0:T(8,128)(2,1)}) %all-gather.5.cloned.1.call-update) | async-done | bytes 4718608 | tf_op jit(solution)/shard_map/all_gather | solution.py:145
  91.1 4.8 fusion.158
  100.0 1.8 copy-done.2
  105.3 1.7 copy-done.3
  110.6 1.7 copy-done.4
  114.2 3.6 convolution_convert_fusion.2
  117.9 85.3 %reduce-scatter.5.cloned.1.call-done = bf16[192,1536]{1,0:T(8,128)(2,1)} async-done(((bf16[1536,1536]{1,0:T(8,128)(2,1)}), bf16[192,1536]{1,0:T(8,128)(2,1)}) %reduce-scatter.5.cloned.1.call-update) | async-done | bytes 589840 | tf_op jit(solution)/shard_map/reduce_scatter | solution.py:185
  204.7 2.3 multiply_convert_fusion.3
  208.1 74.4 %all-gather.7.cloned.1.call-done = bf16[1536,1536]{1,0:T(8,128)(2,1)} async-done(((bf16[192,1536]{1,0:T(8,128)(2,1)}), bf16[1536,1536]{1,0:T(8,128)(2,1)}) %all-gather.7.cloned.1.call-update) | async-done | bytes 4718608 | tf_op jit(solution)/shard_map/all_gather | solution.py:194
  282.4 9.3 %fusion.19 = f32[2,1536,512]{2,1,0:T(8,128)} fusion(bf16[2,1536,512]{2,1,0:T(8,128)(2,1)S(1)} %copy-done, bf16[1536,1536]{1,0:T(8,128)(2,1)} %all-gather.7.cloned.1.call-done), kind=kOutput, calls=%fused_computation.41 | convolution fusion | flops 4831838208 | bytes 14155776 | tf_op jit(solution)/shard_map/td,cdf->ctf/dot_general | solution.py:195
  291.8 66.6 %all-gather.9.cloned.1.call-done = bf16[1536,1536]{1,0:T(8,128)(2,1)} async-done(((bf16[192,1536]{1,0:T(8,128)(2,1)}), bf16[1536,1536]{1,0:T(8,128)(2,1)}) %all-gather.9.cloned.1.call-update) | async-done | bytes 4718608 | tf_op jit(solution)/shard_map/all_gather | solution.py:209
  358.3 9.7 %fusion.80 = (bf16[1,1536,512]{2,1,0:T(8,128)(2,1)S(1)}, bf16[1,1536,512]{2,1,0:T(8,128)(2,1)S(1)}, bf16[1536,512]{1,0:T(8,128)(2,1)}) fusion(f32[2,1536,512]{2,1,0:T(8,128)} %fusion.19, bf16[1536,1536]{1,0:T(8,128)(2,1)} %all-gather.9.cloned.1.call-done, bf16[512,1536]{1,0:T(8,128)(2,1)} %param.13), kind=kOutput, calls=%fused_computation.102 | convolution fusion | flops 2427715584 | bytes 17301504 | tf_op jit(solution)/shard_map/dot_general | solution.py:104
  369.7 6.9 bitcast_convert_fusion
  376.7 85.3 %reduce-scatter.9.cloned.1.call-done = bf16[192,1536]{1,0:T(8,128)(2,1)} async-done(((bf16[1536,1536]{1,0:T(8,128)(2,1)}), bf16[192,1536]{1,0:T(8,128)(2,1)}) %reduce-scatter.9.cloned.1.call-update) | async-done | bytes 589840 | tf_op jit(solution)/shard_map/reduce_scatter | solution.py:221
  462.0 1.7 fusion.92
  463.7 2.3 fusion.145
  466.4 75.0 %all-gather.11.cloned.1.call-done = bf16[1536,1536]{1,0:T(8,128)(2,1)} async-done(((bf16[192,1536]{1,0:T(8,128)(2,1)}), bf16[1536,1536]{1,0:T(8,128)(2,1)}) %all-gather.11.cloned.1.call-update) | async-done | bytes 4718608 | tf_op jit(solution)/shard_map/all_gather | solution.py:226
  541.4 4.2 convolution_convert_fusion.6
  546.3 4.2 fusion
  551.0 1.8 fusion.39
  552.9 2.4 fusion.84
  555.2 1.9 convolution_bitcast_fusion
  557.1 6.6 fusion.3
  563.8 6.5 fusion.38
  570.3 2.4 fusion.85
  572.6 1.9 convolution_bitcast_fusion.1
  575.7 3.9 fusion.6
  582.2 4.5 fusion.37
  591.9 4.4 convolution_convert_fusion
  597.7 5.7 convolution_convert_fusion.1
  603.5 1.7 copy-done.55
  605.2 9.1 %fusion.25 = bf16[2,1536,512]{1,2,0:T(8,128)(2,1)} fusion(bf16[1536,1536]{1,0:T(8,128)(2,1)} %all-gather.7.cloned.1.call-done, bf16[1,1536,512]{2,1,0:T(8,128)(2,1)} %copy-done.56, bf16[1,1536,512]{2,1,0:T(8,128)(2,1)S(1)} %copy-done.55), kind=kOutput, calls=%fused_computation.43 | convolution fusion | flops 4834983936 | bytes 11010048 | tf_op jit(solution)/shard_map/td,ctf->cdf/dot_general | solution.py:215
  614.2 4.8 copy.160
  619.0 2.2 copy.162
  621.2 7.9 all_to_all.45
  629.2 4.4 reduce_sum.235
  633.5 3.5 convolution_convert_fusion.5
  638.6 3.9 all-to-all-start.2
  642.5 5.5 convolution_convert_fusion.4
  648.1 5.1 all_to_all.46
  653.3 4.3 all-to-all-start.5
  657.6 6.7 convolution_convert_fusion.3
  665.4 2.4 reduce_sum.231
  667.9 23.5 %reduce-scatter.11.cloned.1.call-done = bf16[192,1536]{1,0:T(8,128)(2,1)} async-done(((bf16[1536,1536]{1,0:T(8,128)(2,1)}), bf16[192,1536]{1,0:T(8,128)(2,1)}) %reduce-scatter.11.cloned.1.call-update) | async-done | bytes 589840 | tf_op jit(solution)/shard_map/reduce_scatter | solution.py:270
  691.4 1.6 fusion.95
  693.0 4.5 all-to-all-start.3
  697.6 2.7 pad_maximum_fusion.3
  700.3 3.3 reshape.738
  703.6 3.3 copy.163
  706.9 3.1 copy.164
  710.0 8.3 %all_to_all.47 = bf16[2,8,514,96]{2,3,1,0:T(8,128)(2,1)S(1)} all-to-all(bf16[2,8,514,96]{2,3,1,0:T(8,128)(2,1)} %copy.164), channel_id=1, replica_groups=mesh['dp_0'=4,'dp_1'=2,'dp_2'=2,'tensor'=8] {'dp_2'}, dimensions={0} | all-to-all | bytes 3158016 | tf_op jit(solution)/shard_map/all_to_all | solution.py:25
  718.2 5.4 all-to-all-start.1
  723.7 1.6 reduce_sum.239
  725.3 8.2 %all-to-all-done.1 = bf16[8,96,384]{2,1,0:T(8,128)(2,1)S(1)} async-done(((bf16[8,96,384]{2,1,0:T(8,128)(2,1)}), bf16[8,96,384]{2,1,0:T(8,128)(2,1)S(1)}, u32[]{:S(2)}, u32[]{:S(2)}) %all-to-all-start.1) | async-done | bytes 589856 | tf_op jit(solution)/shard_map/all_to_all | solution.py:33
  733.6 4.9 all-to-all-start.7
  738.5 2.4 convert_reduce_fusion
  742.3 10.9 %all-to-all-done.7 = bf16[8,514,96]{1,2,0:T(8,128)(2,1)} async-done(((bf16[8,514,96]{1,2,0:T(8,128)(2,1)}), bf16[8,514,96]{1,2,0:T(8,128)(2,1)}, u32[]{:S(2)}, u32[]{:S(2)}) %all-to-all-start.7) | async-done | bytes 789536 | tf_op jit(solution)/shard_map/all_to_all | solution.py:33
  753.2 1.5 convert_reduce_fusion.1
  755.4 3.4 all-to-all-start.8
  758.8 42.3 %reduce-scatter.7.cloned.1.call-done = bf16[192,1536]{1,0:T(8,128)(2,1)} async-done(((bf16[1536,1536]{1,0:T(8,128)(2,1)}), bf16[192,1536]{1,0:T(8,128)(2,1)}) %reduce-scatter.7.cloned.1.call-update) | async-done | bytes 589840 | tf_op jit(solution)/shard_map/reduce_scatter | solution.py:201
  801.1 4.1 fusion.88
  (201 shorter events, 40.1 us)
Async XLA Ops:
  7.2 275.3 %copy-start = (bf16[2,1536,512]{2,1,0:T(8,128)(2,1)S(1)}, bf16[2,1536,512]{2,1,0:T(8,128)(2,1)}, u32[]{:S(2)}) copy-start(bf16[2,1536,512]{2,1,0:T(8,128)(2,1)} %param.12) | copy-start | bytes 9437188
  7.2 83.9 %all-gather.5.cloned.1.call-start = ((), (), s32[]{:S(2)}) async-start(), calls=%async_computation.13 | async-start | bytes 5308416 | tf_op jit(solution)/shard_map/all_gather | solution.py:145
  12.2 191.0 %reduce-scatter.5.cloned.1.call-start = ((), (), s32[]{:S(2)}) async-start(), calls=%async_computation.14 | async-start | bytes 5308416 | tf_op jit(solution)/shard_map/reduce_scatter | solution.py:185
  91.1 6.4 copy-start.15
  91.1 6.4 copy-start.17
  95.9 14.6 %copy-start.9 = (f32[1536,384]{0,1:T(8,128)}, f32[1536,384]{0,1:T(8,128)S(1)}, u32[]{:S(2)}) copy-start(f32[1536,384]{0,1:T(8,128)S(1)} %fusion.158) | copy-start | bytes 7077892
  95.9 1.8 copy-start.35
  97.5 10.7 %copy-start.21 = (bf16[1536,48]{0,1:T(8,128)(2,1)}, bf16[1536,48]{0,1:T(8,128)(2,1)S(1)}, u32[]{:S(2)}) copy-start(bf16[1536,48]{0,1:T(8,128)(2,1)S(1)} %get-tuple-element.26) | copy-start | bytes 442372
  97.5 10.7 %copy-start.23 = (bf16[1536,48]{0,1:T(8,128)(2,1)}, bf16[1536,48]{0,1:T(8,128)(2,1)S(1)}, u32[]{:S(2)}) copy-start(bf16[1536,48]{0,1:T(8,128)(2,1)S(1)} %get-tuple-element.27) | copy-start | bytes 442372
  97.7 10.5 %copy-start.11 = (bf16[1536,1,2,48]{0,3,2,1:T(8,128)(2,1)}, bf16[1536,1,2,48]{0,3,2,1:T(8,128)(2,1)S(1)}, u32[]{:S(2)}) copy-start(bf16[1536,1,2,48]{0,3,2,1:T(8,128)(2,1)S(1)} %get-tuple-element.19) | copy-start | bytes 884740
  99.2 2.7 copy-start.2
  103.0 10.5 %copy-start.48 = (bf16[96,2,512]{2,0,1:T(8,128)(2,1)}, bf16[96,2,512]{2,0,1:T(8,128)(2,1)S(1)}, u32[]{:S(2)}) copy-start(bf16[96,2,512]{2,0,1:T(8,128)(2,1)S(1)} %fusion.97) | copy-start | bytes 589828
  104.4 2.6 copy-start.3
  108.2 5.3 copy-start.50
  109.7 2.6 copy-start.4
  112.3 1.9 copy-start.47
  117.8 164.6 %all-gather.7.cloned.1.call-start = ((), (), s32[]{:S(2)}) async-start(), calls=%async_computation.15 | async-start | bytes 5308416 | tf_op jit(solution)/shard_map/all_gather | solution.py:194
  204.7 259.0 %copy-start.38 = (f32[192]{0:T(256)}, f32[192]{0:T(256)S(1)}, u32[]{:S(2)}) copy-start(f32[192]{0:T(256)S(1)} %add_rsqrt_fusion) | copy-start | bytes 2308
  207.0 151.3 %all-gather.9.cloned.1.call-start = ((), (), s32[]{:S(2)}) async-start(), calls=%async_computation.17 | async-start | bytes 5308416 | tf_op jit(solution)/shard_map/all_gather | solution.py:209
  207.6 254.4 %reduce-scatter.9.cloned.1.call-start = ((), (), s32[]{:S(2)}) async-start(), calls=%async_computation.18 | async-start | bytes 5308416 | tf_op jit(solution)/shard_map/reduce_scatter | solution.py:221
  368.0 1.7 copy-start.56
  376.6 85.4 %copy-start.5 = (bf16[192,1536]{1,0:T(8,128)(2,1)S(1)}, bf16[192,1536]{1,0:T(8,128)(2,1)}, u32[]{:S(2)}) copy-start(bf16[192,1536]{1,0:T(8,128)(2,1)} %param.8) | copy-start | bytes 1769476
  376.6 85.4 %copy-start.6 = (bf16[192,1536]{1,0:T(8,128)(2,1)S(1)}, bf16[192,1536]{1,0:T(8,128)(2,1)}, u32[]{:S(2)}) copy-start(bf16[192,1536]{1,0:T(8,128)(2,1)} %reduce-scatter.5.cloned.1.call-done) | copy-start | bytes 1769476
  376.6 87.1 %copy-start.8 = (bf16[192,1536]{1,0:T(8,128)(2,1)S(1)}, bf16[192,1536]{1,0:T(8,128)(2,1)}, u32[]{:S(2)}) copy-start(bf16[192,1536]{1,0:T(8,128)(2,1)} %param.15) | copy-start | bytes 1769476
  376.6 164.7 %all-gather.11.cloned.1.call-start = ((), (), s32[]{:S(2)}) async-start(), calls=%async_computation.19 | async-start | bytes 5308416 | tf_op jit(solution)/shard_map/all_gather | solution.py:226
  463.7 2.4 copy-start.43
  466.1 225.3 %reduce-scatter.11.cloned.1.call-start = ((), (), s32[]{:S(2)}) async-start(), calls=%async_computation.20 | async-start | bytes 5308416 | tf_op jit(solution)/shard_map/reduce_scatter | solution.py:270
  466.4 79.9 %copy-start.10 = (f32[1536,384]{0,1:T(8,128)S(1)}, f32[1536,384]{0,1:T(8,128)}, u32[]{:S(2)}) copy-start(f32[1536,384]{0,1:T(8,128)} %copy-done.9) | copy-start | bytes 7077892
  546.3 4.3 copy-start.26
  546.3 4.3 slice-start.2
  546.3 4.7 slice-start.3
  551.0 1.8 copy-start.22
  552.9 2.4 copy-start.12
  552.9 4.3 copy-start.28
  557.1 17.4 %slice-start = ((s8[6291456]{0:T(1024)(128)(4,1)}), s8[4194304]{0:T(1024)(128)(4,1)S(1)}, s32[]{:S(2)}) async-start(s8[6291456]{0:T(1024)(128)(4,1)} %bitcast.312), calls=%async_computation.21 | async-start | bytes 8388608
  563.8 10.7 %slice-start.1 = ((s8[6291456]{0:T(1024)(128)(4,1)}), s8[2097152]{0:T(1024)(128)(4,1)S(1)}, s32[]{:S(2)}) async-start(s8[6291456]{0:T(1024)(128)(4,1)} %bitcast.312), calls=%async_computation.22 | async-start | bytes 4194304
  570.2 2.4 copy-start.13
  570.2 4.3 copy-start.25
  574.5 5.1 slice-start.4
  575.7 3.9 slice-start.5
  575.7 3.9 copy-start.29
  582.2 4.6 copy-start.24
  588.1 2.4 copy-start.30
  588.1 2.4 copy-start.31
  588.1 2.5 copy-start.16
  588.1 2.5 copy-start.18
  591.0 5.3 copy-start.32
  596.3 204.7 %reduce-scatter.7.cloned.1.call-start = ((), (), s32[]{:S(2)}) async-start(), calls=%async_computation.16 | async-start | bytes 5308416 | tf_op jit(solution)/shard_map/reduce_scatter | solution.py:201
  629.2 4.4 copy-start.49
  629.2 4.4 copy-start.51
  629.2 4.4 copy-start.53
  638.6 9.5 %all-to-all-start.2 = ((bf16[2,8,192,96]{3,1,2,0:T(8,128)(2,1)}), bf16[2,8,192,96]{3,1,2,0:T(8,128)(2,1)S(1)}, u32[]{:S(2)}, u32[]{:S(2)}) async-start(bf16[2,8,192,96]{3,1,2,0:T(8,128)(2,1)} %copy.156), calls=%async_computation.6 | async-start | bytes 1572864 | tf_op jit(solution)/shard_map/all_to_all | solution.py:25
  653.3 39.7 %all-to-all-start.5 = ((bf16[8,2,96,512]{3,2,1,0:T(8,128)(2,1)}), bf16[8,2,96,512]{3,2,1,0:T(8,128)(2,1)S(1)}, u32[]{:S(2)}, u32[]{:S(2)}) async-start(bf16[8,2,96,512]{3,2,1,0:T(8,128)(2,1)} %reduce_sum.235), calls=%async_computation.9 | async-start | bytes 3145728 | tf_op jit(solution)/shard_map/all_to_all | solution.py:33
  664.2 27.2 %copy-start.37 = (f32[1536]{0:T(1024)S(1)}, f32[1536]{0:T(1024)}, u32[]{:S(2)}) copy-start(f32[1536]{0:T(1024)} %copy-done.36) | copy-start | bytes 18436
  664.2 27.2 %copy-start.41 = (f32[192]{0:T(256)S(1)}, f32[192]{0:T(256)}, u32[]{:S(2)}) copy-start(f32[192]{0:T(256)} %copy-done.40) | copy-start | bytes 2308
  693.0 4.5 copy-start.7
  693.0 17.0 %all-to-all-start.3 = ((bf16[8,192,96]{2,1,0:T(8,128)(2,1)}), bf16[8,192,96]{2,1,0:T(8,128)(2,1)S(1)}, u32[]{:S(2)}, u32[]{:S(2)}) async-start(bf16[8,192,96]{2,1,0:T(8,128)(2,1)} %copy.158), calls=%async_computation.7 | async-start | bytes 786432 | tf_op jit(solution)/shard_map/all_to_all | solution.py:33
  718.2 15.3 %all-to-all-start.1 = ((bf16[8,96,384]{2,1,0:T(8,128)(2,1)}), bf16[8,96,384]{2,1,0:T(8,128)(2,1)S(1)}, u32[]{:S(2)}, u32[]{:S(2)}) async-start(bf16[8,96,384]{2,1,0:T(8,128)(2,1)} %reduce_sum.231), calls=%async_computation.5 | async-start | bytes 1179648 | tf_op jit(solution)/shard_map/all_to_all | solution.py:33
  725.3 75.7 %copy-start.39 = (f32[192]{0:T(256)S(1)}, f32[192]{0:T(256)}, u32[]{:S(2)}) copy-start(f32[192]{0:T(256)} %copy-done.38) | copy-start | bytes 2308
  725.3 75.7 %copy-start.42 = (f32[192]{0:T(256)S(1)}, f32[192]{0:T(256)}, u32[]{:S(2)}) copy-start(f32[192]{0:T(256)} %copy-done.40) | copy-start | bytes 2308
  725.3 75.7 %copy-start.44 = (f32[192]{0:T(256)S(1)}, f32[192]{0:T(256)}, u32[]{:S(2)}) copy-start(f32[192]{0:T(256)} %copy-done.43) | copy-start | bytes 2308
  733.6 19.7 %all-to-all-start.7 = ((bf16[8,514,96]{1,2,0:T(8,128)(2,1)}), bf16[8,514,96]{1,2,0:T(8,128)(2,1)}, u32[]{:S(2)}, u32[]{:S(2)}) async-start(bf16[8,514,96]{1,2,0:T(8,128)(2,1)} %reduce_sum.239), calls=%async_computation.11 | async-start | bytes 1966080 | tf_op jit(solution)/shard_map/all_to_all | solution.py:33
  753.2 53.2 %copy-start.1 = (bf16[2,1536,512]{2,1,0:T(8,128)(2,1)S(1)}, bf16[2,1536,512]{2,1,0:T(8,128)(2,1)}, u32[]{:S(2)}) copy-start(bf16[2,1536,512]{2,1,0:T(8,128)(2,1)} %param.12) | copy-start | bytes 9437188
  755.4 50.4 %all-to-all-start.8 = ((f32[8,2,96]{2,1,0:T(2,128)}), f32[8,2,96]{2,1,0:T(2,128)S(1)}, u32[]{:S(2)}, u32[]{:S(2)}) async-start(f32[8,2,96]{2,1,0:T(2,128)} %broadcast_in_dim.68), calls=%async_computation.12 | async-start | bytes 16384 | tf_op jit(solution)/shard_map/all_to_all | solution.py:48
  (13 other events, 14.8 us)
Sparse Core Ops, SparseCore 0:
  12.3 78.7 all-gather.4
  118.0 85.1 reduce-scatter.4
  207.2 75.2 all-gather.6
  284.6 73.6 all-gather.8
  376.8 85.2 reduce-scatter.8
  466.2 75.0 all-gather.10
  596.5 94.8 reduce-scatter.10
  695.3 105.7 reduce-scatter.6
where the time goes:
time: 819 us; the launch traced here: 814 us
  waiting for transfers between devices  544 us (66%)
  matrix products  110 us (13%)
  other arithmetic  60.3 us (7%)
  local copies, waits for them, and re-layouts  35.7 us (4%)
  starting transfers between devices  27.3 us (3%)
  blocking collectives  21.3 us (3%)
  between operations  15.4 us (2%)
    reduce_scatter x1, waiting for transfers between devices, per_device(): lax.psum_scatter(normed_two_part.astype(jnp.bfloat16), 'tensor', scatter_...  85.3 us
    reduce_scatter x1, waiting for transfers between devices, per_device(): lax.psum_scatter(jnp.dot(mixed_heads, out_weight, preferred_element_type=...  85.3 us
    all_gather x1, waiting for transfers between devices, per_device(): lax.all_gather(grad_middle.astype(jnp.bfloat16), 'tensor', axis=0, tiled=...  75 us
    all_gather x1, waiting for transfers between devices, per_device(): normed_two_all = lax.all_gather(normed_two, 'tensor', axis=0, tiled=True)  74.4 us
    all_gather x1, waiting for transfers between devices, per_device(): normed_all = lax.all_gather(normed, 'tensor', axis=0, tiled=True)  71.8 us
    all_gather x1, waiting for transfers between devices, per_device(): upstream_all = lax.all_gather(cotangent, 'tensor', axis=0, tiled=True)  66.6 us
    reduce_scatter x1, waiting for transfers between devices, per_device(): lax.psum_scatter(jnp.dot(activated, down_weight, preferred_element_type=j...  42.3 us
    reduce_scatter x1, waiting for transfers between devices, per_device(): lax.psum_scatter(normed_part.astype(jnp.bfloat16), 'tensor', scatter_dime...  23.5 us
  transfers between devices with their start and end apart: 14, of which 10 were waited for; matrix products, arithmetic and copies ran while one was open for 11% of the time, Pallas kernels for 0%

commit v1 on v0

v1 whole, which is shorter than its diff:
```python
import functools

import jax
import jax.numpy as jnp
import numpy as np
from jax import lax
from jax.experimental import pallas as pl
from jax.experimental.pallas import tpu as pltpu
from jax.sharding import Mesh
from jax.sharding import PartitionSpec as P

HEAD_SIZE = 96
BLOCK = 128
DP = ("x", "yl", "c")
TENSOR = ("yh", "z")
ALL = DP + TENSOR
SIZES = {"x": 4, "yl": 2, "c": 2, "yh": 2, "z": 4}
MESH = pl.DeviceIdType.MESH

EPSILON = 1e-05
THETA = 100000.0
masked_score = -1e30


def layout(lengths, total_rows):
    padded_rows = (lengths + BLOCK - 1) // BLOCK * BLOCK
    starts = jnp.cumsum(padded_rows, dtype=jnp.int32) - padded_rows
    places = jnp.arange(total_rows, dtype=jnp.int32)[:, None]
    inside = (places >= starts[None, :]) & (places < (starts + lengths)[None, :])
    slot_ids = jnp.arange(lengths.shape[0], dtype=jnp.int32)
    segment = jnp.sum(jnp.where(inside, slot_ids[None, :], 0), axis=1, dtype=jnp.int32)
    offset = jnp.sum(jnp.where(inside, starts[None, :], 0), axis=1, dtype=jnp.int32)
    anywhere = jnp.any(inside, axis=1)
    positions = places[:, 0] - offset
    segment = jnp.where(anywhere, segment, lengths.shape[0] + places[:, 0])
    return (segment, positions)


def angles(positions):
    exponent = jnp.arange(0, HEAD_SIZE, 2, dtype=jnp.float32) / HEAD_SIZE
    inverse = jnp.power(THETA, -exponent)
    phases = positions.astype(jnp.float32)[:, None] * inverse[None, :]
    return (jnp.cos(phases), jnp.sin(phases))


def rotate(values, cos_part, sin_part):
    half_width = values.shape[-1] // 2
    first_half = values[..., :half_width]
    second_half = values[..., half_width:]
    return jnp.concatenate(
        [
            first_half * cos_part - second_half * sin_part,
            second_half * cos_part + first_half * sin_part,
        ],
        axis=-1,
    )


def unrotate(values, cos_part, sin_part):
    return rotate(values, cos_part, -sin_part)


def times_transposed(left, right):
    return lax.dot_general(
        left, right, (((1,), (1,)), ((), ())), preferred_element_type=jnp.float32
    )


def transposed_times(left, right):
    return lax.dot_general(
        left, right, (((0,), (0,)), ((), ())), preferred_element_type=jnp.float32
    )


def normalize(values):
    scale = lax.rsqrt(jnp.mean(values * values, axis=-1, keepdims=True) + EPSILON)
    return (values * scale, scale)


def norm_back(grad_out, normalized, scale, gain_row):
    scaled = grad_out * gain_row
    return scale * (scaled - normalized * jnp.mean(scaled * normalized, axis=-1, keepdims=True))


def permutation(axes, move):
    shape = [SIZES[a] for a in axes]
    pairs = []
    for source in range(int(np.prod(shape))):
        place = dict(zip(axes, np.unravel_index(source, shape)))
        goal = move(place)
        pairs.append((source, int(np.ravel_multi_index([goal[a] for a in axes], shape))))
    return pairs


def to_other_core(value):
    return lax.ppermute(value, "c", [(0, 1), (1, 0)])


def to_cross(value):
    axes = ("yl", "yh")
    pairs = permutation(axes, lambda p: {"yl": 1 - p["yl"], "yh": 1 - p["yh"]})
    return lax.ppermute(value, axes, pairs)


def to_other_yl(value):
    return lax.ppermute(value, "yl", [(0, 1), (1, 0)])


def barrier_with(partners):
    barrier = pltpu.get_barrier_semaphore()
    for partner in partners:
        pl.semaphore_signal(barrier, inc=1, device_id=partner, device_id_type=MESH)
    pl.semaphore_wait(barrier, len(partners))


def gather_kernel(both, x_ref, o_ref, send_sem, recv_sem, local_sem):
    yh, z = lax.axis_index("yh"), lax.axis_index("z")
    after, before = lax.rem(z + 1, 4), lax.rem(z + 3, 4)
    other = 1 - yh
    right, left, across = {"z": after}, {"z": before}, {"yh": other}
    half = x_ref.shape[0] // 2
    lower, upper = pl.ds(0, half), pl.ds(half, half)
    whole = pl.ds(0, 2 * half)
    barrier_with([right, left, across] if both else [right, left])

    def place(block_yh, block_z, rows):
        if both:
            return o_ref.at[block_yh, block_z, rows]
        return o_ref.at[block_z, rows]

    def sent(slot, source, block_yh, block_z, rows, device):
        copy = pltpu.make_async_remote_copy(
            src_ref=source,
            dst_ref=place(block_yh, block_z, rows),
            send_sem=send_sem.at[slot],
            recv_sem=recv_sem.at[slot],
            device_id=device,
            device_id_type=MESH,
        )
        copy.start()
        return copy

    def passed(slot, block_yh, block_z, rows, device):
        return sent(slot, place(block_yh, block_z, rows), block_yh, block_z, rows, device)

    own = pltpu.make_async_copy(x_ref, place(yh, z, whole), local_sem)
    own.start()
    to_right = sent(0, x_ref, yh, z, whole, right)
    to_left = sent(1, x_ref, yh, z, whole, left)
    copies = [to_right, to_left]
    if both:
        to_across = sent(2, x_ref, yh, z, whole, across)
        copies.append(to_across)
    to_right.wait_recv()
    last = [passed(3, yh, before, lower, right)]
    to_left.wait_recv()
    last.append(passed(4, yh, after, upper, left))
    if both:
        to_across.wait_recv()
        far_right = passed(5, other, z, whole, right)
        far_left = passed(6, other, z, whole, left)
        copies += [far_right, far_left]
        far_right.wait_recv()
        last.append(passed(7, other, before, lower, right))
        far_left.wait_recv()
        last.append(passed(8, other, after, upper, left))
    for copy in last:
        copy.wait_recv()
    for copy in copies + last:
        copy.wait_send()
    own.wait()


def gathered(value, both, collective_id, name):
    blocks = (2, 4) if both else (4,)
    out = pl.pallas_call(
        functools.partial(gather_kernel, both),
        out_shape=jax.ShapeDtypeStruct((*blocks, *value.shape), value.dtype),
        in_specs=[pl.BlockSpec(memory_space=pl.ANY)],
        out_specs=pl.BlockSpec(memory_space=pl.ANY),
        scratch_shapes=[
            pltpu.SemaphoreType.DMA((9,)),
            pltpu.SemaphoreType.DMA((9,)),
            pltpu.SemaphoreType.DMA,
        ],
        compiler_params=pltpu.CompilerParams(collective_id=collective_id, has_side_effects=True),
        name=name,
    )(value)
    return out.reshape(-1, value.shape[-1])


def exchange_kernel(x_ref, o_ref, send_sem, recv_sem, local_sem):
    me = lax.axis_index("yh") * 4 + lax.axis_index("z")
    partners = []
    for step in range(1, 8):
        goal = lax.rem(me + step, 8)
        partners.append((goal, {"yh": lax.div(goal, 4), "z": lax.rem(goal, 4)}))
    barrier_with([device for _, device in partners])
    own = pltpu.make_async_copy(x_ref.at[me], o_ref.at[me], local_sem)
    own.start()
    copies = []
    for step, (goal, device) in enumerate(partners):
        copy = pltpu.make_async_remote_copy(
            src_ref=x_ref.at[goal],
            dst_ref=o_ref.at[me],
            send_sem=send_sem.at[step],
            recv_sem=recv_sem.at[step],
            device_id=device,
            device_id_type=MESH,
        )
        copy.start()
        copies.append(copy)
    for copy in copies:
        copy.wait()
    own.wait()


def exchanged(value, collective_id, name):
    return pl.pallas_call(
        exchange_kernel,
        out_shape=jax.ShapeDtypeStruct(value.shape, value.dtype),
        in_specs=[pl.BlockSpec(memory_space=pl.ANY)],
        out_specs=pl.BlockSpec(memory_space=pl.ANY),
        scratch_shapes=[
            pltpu.SemaphoreType.DMA((7,)),
            pltpu.SemaphoreType.DMA((7,)),
            pltpu.SemaphoreType.DMA,
        ],
        compiler_params=pltpu.CompilerParams(collective_id=collective_id, has_side_effects=True),
        name=name,
    )(value)


def core_slice(value, size, dim):
    return lax.dynamic_slice_in_dim(value, lax.axis_index("c") * size, size, dim)


def picked(value, index, dim):
    return lax.dynamic_index_in_dim(value, index, dim, keepdims=False)


def summed_over_cores(grad):
    core = lax.axis_index("c")
    parts = grad.reshape(*grad.shape[:-2], 8, 2, 96, grad.shape[-1])
    arrived = to_other_core(picked(parts, 1 - core, parts.ndim - 3))
    mine = picked(parts, core, parts.ndim - 3)
    return (mine.astype(jnp.float32) + arrived.astype(jnp.float32)).astype(jnp.bfloat16)


def summed_over_x(grad):
    lead = grad.shape[:-3]
    grad = grad.reshape(*lead, 4, 2 * 96, grad.shape[-1])
    out = lax.psum_scatter(grad, "x", scatter_dimension=len(lead), tiled=True)
    return out.reshape(*lead, 2, 96, grad.shape[-1])


def summed_over_yl(grad):
    yl = lax.axis_index("yl")
    arrived = to_other_yl(picked(grad, 1 - yl, grad.ndim - 3))
    return picked(grad, yl, grad.ndim - 3).astype(jnp.float32) + arrived.astype(jnp.float32)


def per_device(
    tokens,
    seq_lens,
    query_key_value_weight,
    out_weight,
    gate_up_weight,
    down_weight,
    norm_gains,
    cotangent,
):
    shard_rows = tokens.shape[0]
    group_rows = shard_rows * 8
    core, yh = lax.axis_index("c"), lax.axis_index("yh")
    block_rows = 512
    block_count = group_rows // block_rows
    scaling = HEAD_SIZE ** (-0.5)

    hidden = tokens.astype(jnp.float32)
    unit_one, scale_one = normalize(hidden)
    normed = (unit_one * norm_gains[0]).astype(jnp.bfloat16)

    gate_up_half = core_slice(gate_up_weight, 256, 2)
    down_half = core_slice(down_weight, 256, 0)
    gate_up_mine = to_cross(gate_up_half)
    down_mine = to_cross(down_half)
    gate_up_rest = to_other_core(gate_up_mine)
    down_rest = to_other_core(down_mine)
    out_half = core_slice(out_weight, 96, 0)
    out_halves = lax.all_gather(out_half, TENSOR, axis=0, tiled=True)
    out_all = lax.all_gather(out_halves, "c", axis=0, tiled=True)
    upstream_all = lax.all_gather(cotangent, "z", axis=0, tiled=True)

    normed_all = gathered(normed, True, 1, "gather_normed")
    projected_rows = jnp.dot(normed_all, query_key_value_weight, preferred_element_type=jnp.float32)
    projected_rows = projected_rows.reshape(group_rows, 4, HEAD_SIZE)
    segment, positions = layout(seq_lens[0], group_rows)
    cos_part, sin_part = angles(positions)
    queries = rotate(projected_rows[:, 0:2], cos_part[:, None], sin_part[:, None]).astype(
        jnp.bfloat16
    )
    keys_all = rotate(projected_rows[:, 2], cos_part, sin_part).astype(jnp.bfloat16)
    values_all = projected_rows[:, 3].astype(jnp.bfloat16)

    def block_scores(first_row):
        query_block = queries[first_row : first_row + block_rows]
        scores = (
            jnp.einsum("qjd,kd->jqk", query_block, keys_all, preferred_element_type=jnp.float32)
            * scaling
        )
        block_segment = segment[first_row : first_row + block_rows]
        block_positions = positions[first_row : first_row + block_rows]
        allowed = (block_segment[:, None] == segment[None, :]) & (
            positions[None, :] <= block_positions[:, None]
        )
        return (query_block, jnp.where(allowed[None], scores, masked_score))

    attended_list = []
    log_sums = []
    for block_index in range(block_count):
        scores = block_scores(block_index * block_rows)[1]
        row_peak = jnp.max(scores, axis=-1, keepdims=True)
        numerators = jnp.exp(scores - row_peak)
        totals = jnp.sum(numerators, axis=-1, keepdims=True)
        softmax_weights = (numerators / totals).astype(jnp.bfloat16)
        log_sums.append(row_peak + jnp.log(totals))
        attended = jnp.einsum(
            "jqk,kd->qjd", softmax_weights, values_all, preferred_element_type=jnp.float32
        )
        attended_list.append(attended.reshape(block_rows, 2 * HEAD_SIZE))
    mixed_heads = jnp.concatenate(attended_list, axis=0).astype(jnp.bfloat16)

    attended_here = exchanged(mixed_heads.reshape(8, shard_rows, 2 * HEAD_SIZE), 2, "exchange_out")
    attended_here = jnp.transpose(
        attended_here.reshape(8, shard_rows, 2, HEAD_SIZE), (1, 2, 0, 3)
    ).reshape(shard_rows, 16 * HEAD_SIZE)
    branch = jnp.dot(attended_here, out_all, preferred_element_type=jnp.float32)
    middle = hidden + branch
    unit_two, scale_two = normalize(middle)
    normed_two = (unit_two * norm_gains[1]).astype(jnp.bfloat16)
    normed_two_all = gathered(normed_two, False, 3, "gather_normed_two")

    in_order = core == 0
    gate_up_all = jnp.concatenate(
        [
            gate_up_weight,
            jnp.where(in_order, gate_up_mine, gate_up_rest),
            jnp.where(in_order, gate_up_rest, gate_up_mine),
        ],
        axis=2,
    )
    down_all = jnp.concatenate(
        [
            down_weight,
            jnp.where(in_order, down_mine, down_rest),
            jnp.where(in_order, down_rest, down_mine),
        ],
        axis=0,
    )
    gate_up = jnp.einsum(
        "td,cdf->ctf", normed_two_all, gate_up_all, preferred_element_type=jnp.float32
    )
    sigmoid_gate = jax.nn.sigmoid(gate_up[0])
    silu_gate = gate_up[0] * sigmoid_gate
    activated = (silu_gate * gate_up[1]).astype(jnp.bfloat16)
    upstream = cotangent.astype(jnp.float32)
    grad_act = times_transposed(upstream_all, down_all)
    grad_gate = grad_act * gate_up[1] * sigmoid_gate * (1.0 + gate_up[0] * (1.0 - sigmoid_gate))
    grad_upper = grad_act * silu_gate
    grad_gate_up = jnp.stack([grad_gate, grad_upper]).astype(jnp.bfloat16)
    normed_two_part = jnp.einsum(
        "ctf,cdf->td", grad_gate_up, gate_up_all, preferred_element_type=jnp.float32
    ).astype(jnp.bfloat16)
    grad_normed_two = lax.psum_scatter(
        normed_two_part, "z", scatter_dimension=0, tiled=True
    ).astype(jnp.float32)
    activated, normed_two_all, upstream_all, normed_two_part = lax.optimization_barrier(
        (activated, normed_two_all, upstream_all, normed_two_part)
    )
    ffn_out = lax.psum_scatter(
        jnp.dot(activated, down_all, preferred_element_type=jnp.float32).astype(jnp.bfloat16),
        "z",
        scatter_dimension=0,
        tiled=True,
    ).astype(jnp.float32)
    mixed = (middle + ffn_out).astype(jnp.bfloat16)
    down_grad = transposed_times(upstream_all, activated).astype(jnp.bfloat16)
    gate_up_grad = jnp.einsum(
        "td,ctf->cdf", normed_two_all, grad_gate_up, preferred_element_type=jnp.float32
    ).astype(jnp.bfloat16)
    ffn_grad = jnp.concatenate([gate_up_grad, down_grad[None]], axis=0)

    grad_middle = upstream + norm_back(grad_normed_two, unit_two, scale_two, norm_gains[1])
    grad_branch = grad_middle.astype(jnp.bfloat16)
    grad_heads = times_transposed(grad_branch, out_all).astype(jnp.bfloat16)
    grad_heads = jnp.transpose(
        grad_heads.reshape(shard_rows, 2, 8, HEAD_SIZE), (2, 0, 1, 3)
    ).reshape(8, shard_rows, 2 * HEAD_SIZE)
    grad_heads = exchanged(grad_heads, 4, "exchange_grad").reshape(group_rows, 2, HEAD_SIZE)
    out_grad = transposed_times(grad_branch, attended_here).astype(jnp.bfloat16)

    key_grad = jnp.zeros((group_rows, HEAD_SIZE), jnp.float32)
    value_grad = jnp.zeros((group_rows, HEAD_SIZE), jnp.float32)
    query_grads = []
    for block_index in range(block_count):
        first_row = block_index * block_rows
        query_block, scores = block_scores(first_row)
        softmax_weights = jnp.exp(scores - log_sums[block_index])
        soft_low = softmax_weights.astype(jnp.bfloat16)
        grad_block = grad_heads[first_row : first_row + block_rows]
        grad_weights = jnp.einsum(
            "qjd,kd->jqk", grad_block, values_all, preferred_element_type=jnp.float32
        )
        centered = jnp.sum(softmax_weights * grad_weights, axis=-1, keepdims=True)
        grad_scores = (softmax_weights * (grad_weights - centered)).astype(jnp.bfloat16)
        query_grads.append(
            jnp.einsum("jqk,kd->qjd", grad_scores, keys_all, preferred_element_type=jnp.float32)
            * scaling
        )
        key_grad = (
            key_grad
            + jnp.einsum("jqk,qjd->kd", grad_scores, query_block, preferred_element_type=jnp.float32)
            * scaling
        )
        value_grad = value_grad + jnp.einsum(
            "jqk,qjd->kd", soft_low, grad_block, preferred_element_type=jnp.float32
        )
    query_grad = unrotate(
        jnp.concatenate(query_grads, axis=0), cos_part[:, None], sin_part[:, None]
    )
    key_grad = unrotate(key_grad, cos_part, sin_part)
    grad_projected = jnp.concatenate(
        [query_grad, key_grad[:, None], value_grad[:, None]], axis=1
    )
    grad_projected = grad_projected.reshape(group_rows, 4 * HEAD_SIZE).astype(jnp.bfloat16)
    by_z = jnp.transpose(
        grad_projected.reshape(2, 4, shard_rows, 4 * HEAD_SIZE), (1, 0, 2, 3)
    ).reshape(group_rows, 4 * HEAD_SIZE)
    normed_part = times_transposed(by_z, query_key_value_weight).astype(jnp.bfloat16)
    grad_normed = lax.psum_scatter(normed_part, "z", scatter_dimension=0, tiled=True)
    grad_normed = lax.psum_scatter(grad_normed, "yh", scatter_dimension=0, tiled=True).astype(
        jnp.float32
    )
    grad_projected, normed_all, normed_part = lax.optimization_barrier(
        (grad_projected, normed_all, normed_part)
    )
    qkv_grad = transposed_times(normed_all, grad_projected).astype(jnp.bfloat16)
    input_grad = grad_middle + norm_back(grad_normed, unit_one, scale_one, norm_gains[0])

    ffn_grad = summed_over_x(summed_over_cores(ffn_grad))
    ffn_grad = (
        ffn_grad[..., :512].astype(jnp.float32) + to_cross(ffn_grad[..., 512:]).astype(jnp.float32)
    ).astype(jnp.bfloat16)
    ffn_grad = summed_over_yl(ffn_grad)
    out_grad = summed_over_x(summed_over_cores(out_grad))
    out_grad = jnp.transpose(out_grad.reshape(2, 96, 2, 2, 4, 96), (4, 3, 0, 1, 2, 5))
    out_grad = out_grad.reshape(4, 2, 2, 96, 192)
    out_grad = lax.psum_scatter(out_grad, "z", scatter_dimension=0, tiled=True)[0]
    out_grad = (
        picked(out_grad, yh, 0).astype(jnp.float32)
        + to_cross(picked(out_grad, 1 - yh, 0)).astype(jnp.float32)
    ).astype(jnp.bfloat16)
    out_grad = summed_over_yl(out_grad)
    qkv_grad = summed_over_yl(summed_over_x(summed_over_cores(qkv_grad)))

    first = ((lax.axis_index("x") * 2 + lax.axis_index("yl")) * 2 + core) * 96
    rows_one = lax.dynamic_slice_in_dim(query_key_value_weight, first, 96, 0).astype(jnp.float32)
    rows_two = lax.dynamic_slice_in_dim(gate_up_weight, first, 96, 1).astype(jnp.float32)
    gain_rows = lax.dynamic_slice_in_dim(norm_gains, first, 96, 1)
    gains_grad = jnp.stack(
        [
            jnp.sum(qkv_grad * rows_one, axis=1),
            jnp.sum(ffn_grad[0:2] * rows_two, axis=(0, 2)),
        ]
    )
    copies = jnp.broadcast_to(gains_grad, (8, *gains_grad.shape))
    copies = lax.all_to_all(copies, TENSOR, split_axis=0, concat_axis=0, tiled=True)
    gains_grad = jnp.sum(copies, axis=0) / gain_rows
    return (
        mixed,
        input_grad,
        qkv_grad,
        out_grad.T,
        ffn_grad[0:2],
        ffn_grad[2].T,
        gains_grad,
    )


def solution(mesh):
    split = Mesh(mesh.devices.reshape(4, 2, 2, 2, 4), ALL)
    placed = (
        P(ALL, None),
        P(DP, None),
        P(None, TENSOR),
        P(TENSOR, None),
        P(None, None, TENSOR),
        P(TENSOR, None),
        P(),
        P(ALL, None),
    )
    return jax.shard_map(
        per_device,
        mesh=split,
        in_specs=placed,
        out_specs=(
            P(ALL, None),
            P(ALL, None),
            P(DP, TENSOR),
            P(TENSOR, DP),
            P(None, DP, TENSOR),
            P(TENSOR, DP),
            P(None, DP),
        ),
        check_vma=False,
    )
```

time: 819 us -> 665 us (0.81)
  waiting for transfers between devices: 544 us -> 264 us
  Pallas kernels: 0 us -> 108 us
  local copies, waits for them, and re-layouts: 35.7 us -> 62.1 us
  blocking collectives: 21.3 us -> 0 us
    all_gather x4 -> x3, waiting for transfers between devices: 288 us -> 61.1 us  [the longest x1 61.1 us: per_device(): out_halves = lax.all_gather(out_half, TENSOR, axis=0, tiled=True)]
    reduce_scatter x4 -> x7, waiting for transfers between devices: 236 us -> 127 us  [the longest x1 53.3 us: per_device(): lax.psum_scatter(normed_part, 'z', scatter_dimension=0, tiled=True)]
    pallas_call x0 -> x4, Pallas kernels: none -> 108 us  [the longest x2 79.8 us: gathered(): pl.pallas_call(functools.partial(gather_kernel, both), out_shape=jax.Shap...]
    unnamed x8 -> x12, waiting for transfers between devices: 0.64 us -> 66 us
    convert_element_type x1 -> x9, other arithmetic: 2.34 us -> 29.7 us  [the longest x3 15.9 us: per_device(): (softmax_weights * (grad_weights - centered)).astype(jnp.bfloat16)]
    ppermute x0 -> x12, starting transfers between devices: none -> 21.8 us  [the longest x5 11.5 us: to_other_core(): return lax.ppermute(value, 'c', [(0, 1), (1, 0)])]
    all_to_all x6 -> x1, starting transfers between devices: 26.4 us -> 4.89 us  [per_device(): lax.all_to_all(copies, TENSOR, split_axis=0, concat_axis=0, tiled=True)]
    all_to_all x3 -> x0, blocking collectives: 21.3 us -> none  [sent_and_summed(): lax.all_to_all(tiles, axis, split_axis=0, concat_axis=0, tiled=True)]
  transfers between devices with their start and end apart: 14 -> 24, of which waited for: 10 -> 11; matrix products, arithmetic and copies ran while one was open for 11% -> 33% of each run, Pallas kernels for 0% -> 16%
where the time goes in v1:
time: 665 us; the launch traced here: 659 us
  waiting for transfers between devices  264 us (40%)
  matrix products  114 us (17%)
  Pallas kernels  108 us (16%)
  other arithmetic  67.7 us (10%)
  local copies, waits for them, and re-layouts  62.1 us (9%)
  starting transfers between devices  27.9 us (4%)
  between operations  15.3 us (2%)
    pallas_call x2, Pallas kernels, gathered(): pl.pallas_call(functools.partial(gather_kernel, both), out_shape=jax.Shap...  79.8 us
    unnamed x12, waiting for transfers between devices  66 us
    all_gather x1, waiting for transfers between devices, per_device(): out_halves = lax.all_gather(out_half, TENSOR, axis=0, tiled=True)  61.1 us
    reduce_scatter x1, waiting for transfers between devices, per_device(): lax.psum_scatter(normed_part, 'z', scatter_dimension=0, tiled=True)  53.3 us
    reduce_scatter x1, waiting for transfers between devices, per_device(): lax.psum_scatter(jnp.dot(activated, down_all, preferred_element_type=jnp....  29.6 us
    pallas_call x2, Pallas kernels, exchanged(): pl.pallas_call(exchange_kernel, out_shape=jax.ShapeDtypeStruct(value.shap...  27.9 us
    reduce_scatter x1, waiting for transfers between devices, per_device(): lax.psum_scatter(grad_normed, 'yh', scatter_dimension=0, tiled=True)  18.6 us
    dot_general x3, matrix products, per_device(): jnp.einsum('qjd,kd->jqk', grad_block, values_all, preferred_element_type=...  17.8 us
  transfers between devices with their start and end apart: 24, of which 11 were waited for; matrix products, arithmetic and copies ran while one was open for 33% of the time, Pallas kernels for 16%

profile of v1, /device:TPU:1, one launch (start us, length us, event | category | flops | bytes accessed | tf_op | source)
XLA Modules:
  0.0 658.8 jit_solution(18369578559652408216)
XLA Ops:
  9.0 61.1 %all-gather.4.cloned.1.call-done = bf16[768,1536]{1,0:T(8,128)(2,1)} async-done(((bf16[96,1536]{1,0:T(8,128)(2,1)}), bf16[768,1536]{1,0:T(8,128)(2,1)}) %all-gather.4.cloned.1.call-update) | async-done | bytes 2359312 | tf_op jit(solution)/shard_map/all_gather | solution.py:291
  72.1 4.7 copy.156
  76.8 2.8 constant_dynamic-slice_fusion.1
  79.6 1.8 collective-permute-start
  84.7 57.8 %gather_normed.1 = bf16[2,4,192,1536]{3,2,1,0:T(8,128)(2,1)} custom-call(bf16[192,1536]{1,0:T(8,128)(2,1)} %fusion.69.x_ref), custom_call_target="tpu_custom_call" | custom-call | tf_op jit(solution)/shard_map/gather_normed/pallas_call | solution.py:176
  142.6 4.4 fusion.125
  147.0 2.0 fusion.83
  149.2 3.3 compare_and_fusion.2
  157.9 2.5 fusion.118
  163.0 2.2 fusion.78
  167.7 5.4 collective-permute-start.3
  173.2 2.2 fusion.77
  176.6 12.7 %exchange_out.1 = bf16[8,192,192]{2,1,0:T(8,128)(2,1)} custom-call(bf16[8,192,192]{2,1,0:T(8,128)(2,1)} %bitcast.299), custom_call_target="tpu_custom_call" | custom-call | tf_op jit(solution)/shard_map/exchange_out/pallas_call | solution.py:219
  189.3 2.8 reshape.470
  192.2 1.8 copy.201
  194.0 2.0 reshape.471
  195.9 2.6 broadcast_select_fusion.3
  198.6 3.7 broadcast_select_fusion.1
  202.3 3.5 multiply_reduce_fusion.1
  206.8 22.0 %gather_normed_two.1 = bf16[4,192,1536]{2,1,0:T(8,128)(2,1)} custom-call(bf16[192,1536]{1,0:T(8,128)(2,1)} %multiply_convert_fusion.1.x_ref), custom_call_target="tpu_custom_call" | custom-call | tf_op jit(solution)/shard_map/gather_normed_two/pallas_call | solution.py:176
  228.8 9.5 %convolution_bitcast_fusion = f32[2,768,1024]{1,2,0:T(8,128)} fusion(bf16[768,1536,1]{1,0,2:T(8,128)(2,1)} %bitcast.303, bf16[2,1536,256]{1,2,0:T(8,128)(2,1)} %get-tuple-element.29, bf16[2,1536,256]{1,2,0:T(8,128)(2,1)} %get-tuple-element.28, bf16[2,1536,512]{1,2,0:T(8,128)(2,1)} %copy.156), kind=kOutput, calls=%fused_computation.78 | convolution fusion | flops 4850712576 | bytes 14942208 | tf_op jit(solution)/shard_map/td,cdf->ctf/dot_general | solution.py:361
  238.3 9.3 %fusion.64 = (bf16[1,768,1024]{1,2,0:T(8,128)(2,1)S(1)}, bf16[1,768,1024]{1,2,0:T(8,128)(2,1)S(1)}, bf16[768,1024]{0,1:T(8,128)(2,1)}) fusion(f32[2,768,1024]{1,2,0:T(8,128)} %convolution_bitcast_fusion, bf16[768,1536]{1,0:T(8,128)(2,1)} %all-gather.8.cloned.1.call-done, bf16[256,1536]{1,0:T(8,128)(2,1)} %get-tuple-element.35, ...), kind=kOutput, calls=%fused_computation.104 | convolution fusion | flops 2437152768 | bytes 16515072 | tf_op jit(solution)/shard_map/dot_general | solution.py:64
  249.3 6.7 %bitcast_convert_fusion = bf16[768,1536]{1,0:T(8,128)(2,1)} fusion(bf16[2,1536,256]{1,2,0:T(8,128)(2,1)S(1)} %copy-done.31, bf16[2,1536,256]{1,2,0:T(8,128)(2,1)S(1)} %copy-done.30, bf16[2,1536,512]{1,2,0:T(8,128)(2,1)S(1)} %copy-done.14, bf16[1,768,1024]{1,2,0:T(8,128)(2,1)S(1)} %get-tuple-element.26, bf16[1,768,1024]{1,2,0:T(8,128)(2,1)S(1)} %get-tuple-element.25), kind=kOutput, calls=%fused_computation.49 | convolution fusion | flops 4853465088 | bytes 11796480 | tf_op jit(solution)/shard_map/ctf,cdf->td/dot_general | solution.py:372
  256.1 6.4 convolution_convert_fusion.3
  262.6 9.3 %convert_bitcast_fusion = bf16[2,1536,1024]{1,2,0:T(8,128)(2,1)} fusion(bf16[768,1536]{1,0:T(8,128)(2,1)} %bitcast.304, bf16[1,768,1024]{1,2,0:T(8,128)(2,1)} %copy-done.45, bf16[1,768,1024]{1,2,0:T(8,128)(2,1)} %copy-done.44), kind=kOutput, calls=%fused_computation.27 | convolution fusion | flops 4836556800 | bytes 11796480 | tf_op jit(solution)/shard_map/td,ctf->cdf/dot_general | solution.py:389
  271.9 8.6 %copy.173 = bf16[2,1536,1024]{2,1,0:T(8,128)(2,1)} copy(bf16[2,1536,1024]{1,2,0:T(8,128)(2,1)} %convert_bitcast_fusion) | data formatting | bytes 12582912 | tf_op jit(solution)/shard_map/convert_element_type | solution.py:391
  280.5 5.0 convolution_convert_fusion.2
  285.5 2.8 fusion.17
  288.7 5.3 collective-permute-start.9
  295.4 29.6 %reduce-scatter.11.cloned.1.call-done = bf16[192,1536]{1,0:T(8,128)(2,1)} async-done(((bf16[768,1536]{1,0:T(8,128)(2,1)}), bf16[192,1536]{1,0:T(8,128)(2,1)}) %reduce-scatter.11.cloned.1.call-update) | async-done | bytes 589840 | tf_op jit(solution)/shard_map/reduce_scatter | solution.py:381
  325.0 2.8 multiply_add_fusion
  327.8 3.5 convolution_convert_fusion
  337.6 15.2 %exchange_grad.1 = bf16[8,192,192]{2,1,0:T(8,128)(2,1)} custom-call(bf16[8,192,192]{2,1,0:T(8,128)(2,1)} %reshape.474.x_ref), custom_call_target="tpu_custom_call" | custom-call | tf_op jit(solution)/shard_map/exchange_grad/pallas_call | solution.py:219
  352.8 2.6 reshape.504
  356.5 3.4 dynamic-slice_bitcast_fusion
  360.5 6.8 %fusion.1 = (f32[2,512]{1,0:T(2,128)S(1)}, f32[1536,512,2]{1,0,2:T(8,128)}) fusion(f32[2,512,1536]{1,2,0:T(8,128)} %copy-done.2, f32[2,512]{1,0:T(2,128)S(1)} %log_add_fusion, bf16[512,2,96]{0,2,1:T(8,128)(2,1)S(1)} %copy.197, f32[1536,4,96]{0,2,1:T(8,128)} %copy-done.15), kind=kOutput, calls=%fused_computation.11 | convolution fusion | flops 306707456 | bytes 13082624 | tf_op jit(solution)/shard_map/qjd,kd->jqk/dot_general | solution.py:412
  367.3 4.7 fusion.3
  373.1 6.0 fusion.4
  379.1 3.8 fusion.20
  383.4 6.5 fusion.6
  393.8 4.9 fusion.7
  398.8 4.7 fusion.9
  405.1 1.9 fusion.90
  407.1 6.9 %fusion = bf16[3,8,96,1024]{3,2,1,0:T(8,128)(2,1)} fusion(bf16[3,8,96,1024]{3,2,1,0:T(8,128)(2,1)} %collective-permute-done.9, s32[]{:T(128)S(6)} %select_n.125, bf16[2,8,2,96,1024]{4,3,2,1,0:T(8,128)(2,1)S(1)} %bitcast.282, bf16[1,8,2,96,1024]{4,3,2,1,0:T(8,128)(2,1)S(1)} %bitcast.291), kind=kLoop, calls=%fused_computation.5 | loop fusion | flops 11796480 | bytes 18874372 | tf_op jit(solution)/shard_map/convert_element_type | solution.py:247
  415.5 2.6 fusion.68
  418.3 4.1 fusion.38
  426.7 3.7 reshape.505
  430.5 2.5 copy.191
  433.0 6.6 convolution_convert_fusion.1
  439.6 5.0 convolution_convert_fusion.4
  444.9 1.8 collective-permute-done.4
  448.7 2.3 reshape_reshape.3
  453.3 65.1 %all-reduce.3.cloned.1.call-done = bf16[3,4,192,1024]{3,2,1,0:T(8,128)(2,1)} async-done(((bf16[3,4,192,1024]{3,2,1,0:T(8,128)(2,1)}), bf16[3,4,192,1024]{3,2,1,0:T(8,128)(2,1)}) %all-reduce.3.cloned.1.call-update) | async-done | bytes 4718608
  518.4 2.0 constant_dynamic-slice_fusion.4
  520.5 2.5 collective-permute-start.10
  523.0 17.5 %reduce-scatter.19.cloned.1.call-done = bf16[1,192,384]{2,1,0:T(8,128)(2,1)} async-done(((bf16[4,192,384]{2,1,0:T(8,128)(2,1)}), bf16[1,192,384]{2,1,0:T(8,128)(2,1)}) %reduce-scatter.19.cloned.1.call-update) | async-done | bytes 147472 | tf_op jit(solution)/shard_map/reduce_scatter | solution.py:253
  542.7 53.3 %reduce-scatter.15.cloned.1.call-done = bf16[384,1536]{1,0:T(8,128)(2,1)} async-done(((bf16[1536,1536]{1,0:T(8,128)(2,1)}), bf16[384,1536]{1,0:T(8,128)(2,1)}) %reduce-scatter.15.cloned.1.call-update) | async-done | bytes 1179664 | tf_op jit(solution)/shard_map/reduce_scatter | solution.py:441
  599.3 5.0 collective-permute-done.11
  604.4 1.9 multiply_reduce_fusion.2
  606.9 4.9 all-to-all-start
  611.8 7.6 %reduce-scatter.23.cloned.1.call-done = bf16[1,2,2,96,192]{3,4,2,1,0:T(8,128)(2,1)} async-done(((bf16[4,2,2,96,192]{3,4,2,1,0:T(8,128)(2,1)}), bf16[1,2,2,96,192]{3,4,2,1,0:T(8,128)(2,1)}) %reduce-scatter.23.cloned.1.call-update) | async-done | bytes 147472 | tf_op jit(solution)/shard_map/reduce_scatter | solution.py:459
  620.3 2.5 collective-permute-start.7
  629.6 18.6 %reduce-scatter.17.cloned.1.call-done = bf16[192,1536]{1,0:T(8,128)(2,1)} async-done(((bf16[384,1536]{1,0:T(8,128)(2,1)}), bf16[192,1536]{1,0:T(8,128)(2,1)}) %reduce-scatter.17.cloned.1.call-update) | async-done | bytes 589840 | tf_op jit(solution)/shard_map/reduce_scatter | solution.py:442
  649.6 2.4 fusion.73
  (251 shorter events, 64.0 us)
Async XLA Ops:
  7.2 63.1 %copy-start.35 = (bf16[512,1536]{1,0:T(8,128)(2,1)S(1)}, bf16[512,1536]{1,0:T(8,128)(2,1)}, u32[]{:S(2)}) copy-start(bf16[512,1536]{1,0:T(8,128)(2,1)} %param.13) | copy-start | bytes 4718596
  7.2 63.0 %all-gather.4.cloned.1.call-start = ((), (), s32[]{:S(2)}) async-start(), calls=%async_computation.8 | async-start | bytes 2654208 | tf_op jit(solution)/shard_map/all_gather | solution.py:291
  9.0 193.3 %all-gather.6.cloned.1.call-start = ((), (), s32[]{:S(2)}) async-start(), calls=%async_computation.9 | async-start | bytes 7077888 | tf_op jit(solution)/shard_map/all_gather | solution.py:292
  70.2 168.1 %all-gather.8.cloned.1.call-start = ((), (), s32[]{:S(2)}) async-start(), calls=%async_computation.10 | async-start | bytes 2949120 | tf_op jit(solution)/shard_map/all_gather | solution.py:293
  71.2 96.5 %collective-permute-start.2 = (bf16[256,1536]{1,0:T(8,128)(2,1)}, bf16[256,1536]{1,0:T(8,128)(2,1)}, u32[]{:S(2)}, u32[]{:S(2)}) collective-permute-start(bf16[256,1536]{1,0:T(8,128)(2,1)} %constant_dynamic-slice_fusion), channel_id=1, source_target_pairs={{0,20},{4,16},{16,4},{20,0},{1,21},{5,17},{17,5},{21,1},{2,22},{6,... | collective-permute-start | bytes 2359304 | tf_op jit(solution)/shard_map/ppermute | solution.py:102
  76.8 4.7 copy-start.42
  76.8 5.1 copy-start.11
  76.8 5.4 copy-start.41
  76.8 5.5 copy-start.32
  79.6 93.5 %collective-permute-start = (bf16[2,1536,256]{1,2,0:T(8,128)(2,1)}, bf16[2,1536,256]{1,2,0:T(8,128)(2,1)}, u32[]{:S(2)}, u32[]{:S(2)}) collective-permute-start(bf16[2,1536,256]{1,2,0:T(8,128)(2,1)} %constant_dynamic-slice_fusion.1), channel_id=1, source_target_pairs={{0,20},{4,16},{16,4},{20,0},{1,21},{5,17},{17,5},{21,1},{2,22},{6,... | collective-permute-start | bytes 4718600 | tf_op jit(solution)/shard_map/ppermute | solution.py:102
  81.4 212.6 %reduce-scatter.13.cloned.1.call-start = ((), (), s32[]{:S(2)}) async-start(), calls=%async_computation.12 | async-start | bytes 2949120 | tf_op jit(solution)/shard_map/reduce_scatter | solution.py:375
  82.1 60.4 %copy-start.39 = (f32[192]{0:T(256)}, f32[192]{0:T(256)S(1)}, u32[]{:S(2)}) copy-start(f32[192]{0:T(256)S(1)} %add_rsqrt_fusion.1) | copy-start | bytes 2308
  82.2 60.3 %copy-start.37 = (f32[1536]{0:T(1024)}, f32[1536]{0:T(1024)S(1)}, u32[]{:S(2)}) copy-start(f32[1536]{0:T(1024)S(1)} %get-tuple-element.18) | copy-start | bytes 18436
  83.7 58.9 %copy-start.34 = (bf16[1536,384]{0,1:T(8,128)(2,1)S(1)}, bf16[1536,384]{0,1:T(8,128)(2,1)}, u32[]{:S(2)}) copy-start(bf16[1536,384]{0,1:T(8,128)(2,1)} %copy.147) | copy-start | bytes 3538948
  147.0 7.8 %copy-start.15 = (f32[1536,4,96]{0,2,1:T(8,128)}, f32[1536,4,96]{0,2,1:T(8,128)S(1)}, u32[]{:S(2)}) copy-start(f32[1536,4,96]{0,2,1:T(8,128)S(1)} %fusion.125) | copy-start | bytes 7077892
  149.0 4.9 copy-start.17
  149.0 16.4 %copy-start.19 = (bf16[1536,48]{0,1:T(8,128)(2,1)}, bf16[1536,48]{0,1:T(8,128)(2,1)S(1)}, u32[]{:S(2)}) copy-start(bf16[1536,48]{0,1:T(8,128)(2,1)S(1)} %get-tuple-element.51) | copy-start | bytes 442372
  166.8 6.4 copy-start.4
  167.7 28.2 %collective-permute-start.3 = (bf16[256,1536]{1,0:T(8,128)(2,1)}, bf16[256,1536]{1,0:T(8,128)(2,1)}, u32[]{:S(2)}, u32[]{:S(2)}) collective-permute-start(bf16[256,1536]{1,0:T(8,128)(2,1)} %collective-permute-done.2), channel_id=1, source_target_pairs={{0,8},{8,0},{1,9},{9,1},{2,10},{10,2},{3,11},{11,3},{4,12},{12,4},... | collective-permute-start | bytes 2359304 | tf_op jit(solution)/shard_map/ppermute | solution.py:96
  173.1 25.5 %collective-permute-start.1 = (bf16[2,1536,256]{1,2,0:T(8,128)(2,1)}, bf16[2,1536,256]{1,2,0:T(8,128)(2,1)}, u32[]{:S(2)}, u32[]{:S(2)}) collective-permute-start(bf16[2,1536,256]{1,2,0:T(8,128)(2,1)} %collective-permute-done), channel_id=1, source_target_pairs={{0,8},{8,0},{1,9},{9,1},{2,10},{10,2},{3,11},{11,3},{4,12},{12,4},... | collective-permute-start | bytes 4718600 | tf_op jit(solution)/shard_map/ppermute | solution.py:96
  238.3 11.0 %copy-start.14 = (bf16[2,1536,512]{1,2,0:T(8,128)(2,1)S(1)}, bf16[2,1536,512]{1,2,0:T(8,128)(2,1)}, u32[]{:S(2)}) copy-start(bf16[2,1536,512]{1,2,0:T(8,128)(2,1)} %copy.156) | copy-start | bytes 9437188
  238.3 11.0 %copy-start.30 = (bf16[2,1536,256]{1,2,0:T(8,128)(2,1)S(1)}, bf16[2,1536,256]{1,2,0:T(8,128)(2,1)}, u32[]{:S(2)}) copy-start(bf16[2,1536,256]{1,2,0:T(8,128)(2,1)} %get-tuple-element.28) | copy-start | bytes 4718596
  238.3 11.0 %copy-start.31 = (bf16[2,1536,256]{1,2,0:T(8,128)(2,1)S(1)}, bf16[2,1536,256]{1,2,0:T(8,128)(2,1)}, u32[]{:S(2)}) copy-start(bf16[2,1536,256]{1,2,0:T(8,128)(2,1)} %get-tuple-element.29) | copy-start | bytes 4718596
  256.0 68.9 %reduce-scatter.11.cloned.1.call-start = ((), (), s32[]{:S(2)}) async-start(), calls=%async_computation.11 | async-start | bytes 2949120 | tf_op jit(solution)/shard_map/reduce_scatter | solution.py:381
  262.5 186.2 %reduce-scatter.21.cloned.1.call-start = ((), (), s32[]{:S(2)}) async-start(), calls=%async_computation.16 | async-start | bytes 2949120 | tf_op jit(solution)/shard_map/reduce_scatter | solution.py:253
  280.5 5.0 copy-start.5
  288.7 118.3 %collective-permute-start.9 = (bf16[3,8,96,1024]{3,2,1,0:T(8,128)(2,1)}, bf16[3,8,96,1024]{3,2,1,0:T(8,128)(2,1)}, u32[]{:S(2)}, u32[]{:S(2)}) collective-permute-start(bf16[3,8,96,1024]{3,2,1,0:T(8,128)(2,1)} %fusion.17), channel_id=1, source_target_pairs={{0,8},{8,0},{1,9},{9,1},{2,10},{10,2},{3,11},{11,3},{4,12},{12,4},... | collective-permute-start | bytes 14155784 | tf_op jit(solution)/shard_map/ppermute | solution.py:96
  325.0 6.3 slice-start.14
  356.1 11.1 %copy-start.24 = (bf16[512,2,96]{0,2,1:T(8,128)(2,1)}, bf16[512,2,96]{0,2,1:T(8,128)(2,1)S(1)}, u32[]{:S(2)}) copy-start(bf16[512,2,96]{0,2,1:T(8,128)(2,1)S(1)} %copy.197) | copy-start | bytes 589828
  356.3 16.7 %copy-start.26 = (bf16[512,2,96]{0,2,1:T(8,128)(2,1)}, bf16[512,2,96]{0,2,1:T(8,128)(2,1)S(1)}, u32[]{:S(2)}) copy-start(bf16[512,2,96]{0,2,1:T(8,128)(2,1)S(1)} %copy.196) | copy-start | bytes 589828
  356.5 37.3 %copy-start.22 = (bf16[512,2,96]{0,2,1:T(8,128)(2,1)}, bf16[512,2,96]{0,2,1:T(8,128)(2,1)S(1)}, u32[]{:S(2)}) copy-start(bf16[512,2,96]{0,2,1:T(8,128)(2,1)S(1)} %copy.195) | copy-start | bytes 589828
  356.5 10.8 %slice-start = ((s8[6291456]{0:T(1024)(128)(4,1)}), s8[4194304]{0:T(1024)(128)(4,1)S(1)}, s32[]{:S(2)}) async-start(s8[6291456]{0:T(1024)(128)(4,1)} %bitcast.269), calls=%async_computation.19 | async-start | bytes 8388608
  360.0 7.3 %slice-start.1 = ((s8[6291456]{0:T(1024)(128)(4,1)}), s8[2097152]{0:T(1024)(128)(4,1)S(1)}, s32[]{:S(2)}) async-start(s8[6291456]{0:T(1024)(128)(4,1)} %bitcast.269), calls=%async_computation.20 | async-start | bytes 4194304
  360.0 19.1 %collective-permute-start.6 = (bf16[8,96,1536]{2,1,0:T(8,128)(2,1)}, bf16[8,96,1536]{2,1,0:T(8,128)(2,1)}, u32[]{:S(2)}, u32[]{:S(2)}) collective-permute-start(bf16[8,96,1536]{2,1,0:T(8,128)(2,1)} %dynamic-slice_bitcast_fusion), channel_id=1, source_target_pairs={{0,8},{8,0},{1,9},{9,1},{2,10},{10,2},{3,11},{11,3},{4,12},{12,4},... | collective-permute-start | bytes 7077896 | tf_op jit(solution)/shard_map/ppermute | solution.py:96
  360.5 12.6 %slice-start.6 = ((s8[6291456]{0:T(1024)(128)(4,1)}), s8[4194304]{0:T(1024)(128)(4,1)S(1)}, s32[]{:S(2)}) async-start(s8[6291456]{0:T(1024)(128)(4,1)} %bitcast.275), calls=%async_computation.25 | async-start | bytes 8388608
  367.3 5.8 slice-start.7
  372.0 7.2 %copy-start.7 = (bf16[2,512,1536]{1,2,0:T(8,128)(2,1)}, bf16[2,512,1536]{1,2,0:T(8,128)(2,1)S(1)}, u32[]{:S(2)}) copy-start(bf16[2,512,1536]{1,2,0:T(8,128)(2,1)S(1)} %fusion.3) | copy-start | bytes 9437188
  372.0 7.2 %slice-start.12 = ((s8[4718592]{0:T(1024)(128)(4,1)}), s8[4194304]{0:T(1024)(128)(4,1)S(1)}, s32[]{:S(2)}) async-start(s8[4718592]{0:T(1024)(128)(4,1)} %bitcast.284), calls=%async_computation.31 | async-start | bytes 8388608
  373.1 6.0 slice-start.13
  383.0 135.4 %all-reduce.3.cloned.1.call-start = ((), (), s32[]{:S(2)}) async-start(), calls=%async_computation.18 | async-start | bytes 9437184
  383.4 7.6 %copy-start.8 = (bf16[2,512,1536]{1,2,0:T(8,128)(2,1)S(1)}, bf16[2,512,1536]{1,2,0:T(8,128)(2,1)}, u32[]{:S(2)}) copy-start(bf16[2,512,1536]{1,2,0:T(8,128)(2,1)} %copy-done.7) | copy-start | bytes 9437188
  398.8 8.3 %slice-start.10 = ((s8[6291456]{0:T(1024)(128)(4,1)}), s8[4194304]{0:T(1024)(128)(4,1)S(1)}, s32[]{:S(2)}) async-start(s8[6291456]{0:T(1024)(128)(4,1)} %bitcast.280), calls=%async_computation.29 | async-start | bytes 8388608
  398.8 8.3 %slice-start.11 = ((s8[6291456]{0:T(1024)(128)(4,1)}), s8[2097152]{0:T(1024)(128)(4,1)S(1)}, s32[]{:S(2)}) async-start(s8[6291456]{0:T(1024)(128)(4,1)} %bitcast.280), calls=%async_computation.30 | async-start | bytes 4194304
  414.0 8.4 %slice-start.8 = ((s8[6291456]{0:T(1024)(128)(4,1)}), s8[2097152]{0:T(1024)(128)(4,1)S(1)}, s32[]{:S(2)}) async-start(s8[6291456]{0:T(1024)(128)(4,1)} %bitcast.277), calls=%async_computation.27 | async-start | bytes 4194304
  414.0 126.5 %reduce-scatter.19.cloned.1.call-start = ((), (), s32[]{:S(2)}) async-start(), calls=%async_computation.15 | async-start | bytes 737280 | tf_op jit(solution)/shard_map/reduce_scatter | solution.py:253
  418.1 4.2 slice-start.9
  418.2 5.3 slice-start.2
  433.0 6.6 copy-start.16
  444.6 2.1 collective-permute-start.4
  447.7 5.0 copy-start.43
  447.7 148.2 %reduce-scatter.15.cloned.1.call-start = ((), (), s32[]{:S(2)}) async-start(), calls=%async_computation.13 | async-start | bytes 5898240 | tf_op jit(solution)/shard_map/reduce_scatter | solution.py:441
  448.5 170.9 %reduce-scatter.23.cloned.1.call-start = ((), (), s32[]{:S(2)}) async-start(), calls=%async_computation.17 | async-start | bytes 983040 | tf_op jit(solution)/shard_map/reduce_scatter | solution.py:459
  452.6 195.6 %reduce-scatter.17.cloned.1.call-start = ((), (), s32[]{:S(2)}) async-start(), calls=%async_computation.14 | async-start | bytes 1769472 | tf_op jit(solution)/shard_map/reduce_scatter | solution.py:442
  520.5 75.5 %collective-permute-start.10 = (bf16[3,2,96,512]{3,2,1,0:T(8,128)(2,1)S(1)}, bf16[3,2,96,512]{3,2,1,0:T(8,128)(2,1)S(1)}, u32[]{:S(2)}, u32[]{:S(2)}) collective-permute-start(bf16[3,2,96,512]{3,2,1,0:T(8,128)(2,1)S(1)} %slice.165), channel_id=1, source_target_pairs={{0,20},{4,16},{16,4},{20,0},{1,21},{5,17},{17,5},{21,1},{2,22},{6,... | collective-permute-start | bytes 1769480 | tf_op jit(solution)/shard_map/ppermute | solution.py:102
  540.5 57.0 %copy-start.36 = (bf16[1,192,384]{2,1,0:T(8,128)(2,1)S(1)}, bf16[1,192,384]{2,1,0:T(8,128)(2,1)}, u32[]{:S(2)}) copy-start(bf16[1,192,384]{2,1,0:T(8,128)(2,1)} %reduce-scatter.19.cloned.1.call-done) | copy-start | bytes 442372
  541.5 56.1 %collective-permute-start.5 = (bf16[96,384]{1,0:T(8,128)(2,1)S(1)}, bf16[96,384]{1,0:T(8,128)(2,1)}, u32[]{:S(2)}, u32[]{:S(2)}) collective-permute-start(bf16[96,384]{1,0:T(8,128)(2,1)S(1)} %dynamic-slice_bitcast_fusion.4), channel_id=1, source_target_pairs={{0,16},{16,0},{1,17},{17,1},{2,18},{18,2},{3,19},{19,3},{4,20},{20... | collective-permute-start | bytes 221192 | tf_op jit(solution)/shard_map/ppermute | solution.py:106
  596.0 52.2 %copy-start.38 = (f32[1536]{0:T(1024)S(1)}, f32[1536]{0:T(1024)}, u32[]{:S(2)}) copy-start(f32[1536]{0:T(1024)} %copy-done.37) | copy-start | bytes 18436
  596.0 52.2 %copy-start.40 = (f32[192]{0:T(256)S(1)}, f32[192]{0:T(256)}, u32[]{:S(2)}) copy-start(f32[192]{0:T(256)} %copy-done.39) | copy-start | bytes 2308
  596.2 53.4 %copy-start.10 = (f32[192,1536]{1,0:T(8,128)S(1)}, f32[192,1536]{1,0:T(8,128)}, u32[]{:S(2)}) copy-start(f32[192,1536]{1,0:T(8,128)} %copy-done.9) | copy-start | bytes 3538948
  596.3 8.0 %collective-permute-start.11 = (bf16[3,96,512]{2,1,0:T(8,128)(2,1)S(1)}, bf16[3,96,512]{2,1,0:T(8,128)(2,1)S(1)}, u32[]{:S(2)}, u32[]{:S(2)}) collective-permute-start(bf16[3,96,512]{2,1,0:T(8,128)(2,1)S(1)} %dynamic-slice_bitcast_fusion.2), channel_id=1, source_target_pairs={{0,16},{16,0},{1,17},{17,1},{2,18},{18,2},{3,19},{19,3},{4,20},{20... | collective-permute-start | bytes 884744 | tf_op jit(solution)/shard_map/ppermute | solution.py:106
  604.4 47.7 %copy-start.1 = (bf16[192,1536]{1,0:T(8,128)(2,1)S(1)}, bf16[192,1536]{1,0:T(8,128)(2,1)}, u32[]{:S(2)}) copy-start(bf16[192,1536]{1,0:T(8,128)(2,1)} %param.11) | copy-start | bytes 1769476
  606.9 16.6 %all-to-all-start = ((f32[8,2,96]{2,1,0:T(2,128)}), f32[8,2,96]{2,1,0:T(2,128)S(1)}, u32[]{:S(2)}, u32[]{:S(2)}) async-start(f32[8,2,96]{2,1,0:T(2,128)} %broadcast_in_dim.66), calls=%async_computation.7 | async-start | bytes 16384 | tf_op jit(solution)/shard_map/all_to_all | solution.py:478
  620.3 4.7 collective-permute-start.7
  625.9 3.0 collective-permute-start.8
  (22 other events, 54.9 us)
Sparse Core Ops, SparseCore 0:
  10.9 59.2 all-gather.3
  71.8 15.6 all-gather.5
  89.2 52.6 all-gather.7
  256.1 34.8 reduce-scatter.12
  293.3 31.6 reduce-scatter.10
  383.1 31.8 reduce-scatter.20
  417.3 101.0 all-reduce.2
  520.8 19.6 reduce-scatter.18
  542.9 52.9 reduce-scatter.14
  598.2 21.0 reduce-scatter.22
  621.7 26.4 reduce-scatter.16

commit v2 on v1

v2 whole, which is shorter than its diff:
```python
import functools

import jax
import jax.numpy as jnp
import numpy as np
from jax import lax
from jax.experimental import pallas as pl
from jax.experimental.pallas import tpu as pltpu
from jax.sharding import Mesh
from jax.sharding import PartitionSpec as P

HEAD_SIZE = 96
BLOCK = 128
DP = ("x", "yl", "c")
TENSOR = ("yh", "z")
ALL = DP + TENSOR
SIZES = {"x": 4, "yl": 2, "c": 2, "yh": 2, "z": 4}
MESH = pl.DeviceIdType.MESH

EPSILON = 1e-05
THETA = 100000.0
masked_score = -1e30


def layout(lengths, total_rows):
    padded_rows = (lengths + BLOCK - 1) // BLOCK * BLOCK
    starts = jnp.cumsum(padded_rows, dtype=jnp.int32) - padded_rows
    places = jnp.arange(total_rows, dtype=jnp.int32)[:, None]
    inside = (places >= starts[None, :]) & (places < (starts + lengths)[None, :])
    offset = jnp.sum(jnp.where(inside, starts[None, :], 0), axis=1, dtype=jnp.int32)
    anywhere = jnp.any(inside, axis=1)
    positions = places[:, 0] - offset
    first = jnp.where(anywhere, offset, places[:, 0])
    return (first, positions)


def angles(positions):
    exponent = jnp.arange(0, HEAD_SIZE, 2, dtype=jnp.float32) / HEAD_SIZE
    inverse = jnp.power(THETA, -exponent)
    phases = positions.astype(jnp.float32)[:, None] * inverse[None, :]
    return (jnp.cos(phases), jnp.sin(phases))


def spread_columns(weight):
    halves = weight.reshape(weight.shape[0], -1, HEAD_SIZE // 2)
    return jnp.pad(halves, ((0, 0), (0, 0), (0, 16))).reshape(weight.shape[0], -1)


def packed_columns(grad):
    return grad.reshape(grad.shape[0], -1, 64)[:, :, :48].reshape(grad.shape[0], -1)


def times_transposed(left, right):
    return lax.dot_general(
        left, right, (((1,), (1,)), ((), ())), preferred_element_type=jnp.float32
    )


def transposed_times(left, right):
    return lax.dot_general(
        left, right, (((0,), (0,)), ((), ())), preferred_element_type=jnp.float32
    )


def normalize(values):
    scale = lax.rsqrt(jnp.mean(values * values, axis=-1, keepdims=True) + EPSILON)
    return (values * scale, scale)


def norm_back(grad_out, normalized, scale, gain_row):
    scaled = grad_out * gain_row
    return scale * (scaled - normalized * jnp.mean(scaled * normalized, axis=-1, keepdims=True))


def permutation(axes, move):
    shape = [SIZES[a] for a in axes]
    pairs = []
    for source in range(int(np.prod(shape))):
        place = dict(zip(axes, np.unravel_index(source, shape)))
        goal = move(place)
        pairs.append((source, int(np.ravel_multi_index([goal[a] for a in axes], shape))))
    return pairs


def to_other_core(value):
    return lax.ppermute(value, "c", [(0, 1), (1, 0)])


def to_cross(value):
    axes = ("yl", "yh")
    pairs = permutation(axes, lambda p: {"yl": 1 - p["yl"], "yh": 1 - p["yh"]})
    return lax.ppermute(value, axes, pairs)


def to_other_yl(value):
    return lax.ppermute(value, "yl", [(0, 1), (1, 0)])


def barrier_with(partners):
    barrier = pltpu.get_barrier_semaphore()
    for partner in partners:
        pl.semaphore_signal(barrier, inc=1, device_id=partner, device_id_type=MESH)
    pl.semaphore_wait(barrier, len(partners))


def gather_kernel(both, x_ref, o_ref, send_sem, recv_sem, local_sem):
    yh, z = lax.axis_index("yh"), lax.axis_index("z")
    after, before = lax.rem(z + 1, 4), lax.rem(z + 3, 4)
    other = 1 - yh
    right, left, across = {"z": after}, {"z": before}, {"yh": other}
    half = x_ref.shape[0] // 2
    lower, upper = pl.ds(0, half), pl.ds(half, half)
    whole = pl.ds(0, 2 * half)
    barrier_with([right, left, across] if both else [right, left])

    def place(block_yh, block_z, rows):
        if both:
            return o_ref.at[block_yh, block_z, rows]
        return o_ref.at[block_z, rows]

    def sent(slot, source, block_yh, block_z, rows, device):
        copy = pltpu.make_async_remote_copy(
            src_ref=source,
            dst_ref=place(block_yh, block_z, rows),
            send_sem=send_sem.at[slot],
            recv_sem=recv_sem.at[slot],
            device_id=device,
            device_id_type=MESH,
        )
        copy.start()
        return copy

    def passed(slot, block_yh, block_z, rows, device):
        return sent(slot, place(block_yh, block_z, rows), block_yh, block_z, rows, device)

    own = pltpu.make_async_copy(x_ref, place(yh, z, whole), local_sem)
    own.start()
    to_right = sent(0, x_ref, yh, z, whole, right)
    to_left = sent(1, x_ref, yh, z, whole, left)
    copies = [to_right, to_left]
    if both:
        to_across = sent(2, x_ref, yh, z, whole, across)
        copies.append(to_across)
    to_right.wait_recv()
    last = [passed(3, yh, before, lower, right)]
    to_left.wait_recv()
    last.append(passed(4, yh, after, upper, left))
    if both:
        to_across.wait_recv()
        far_right = passed(5, other, z, whole, right)
        far_left = passed(6, other, z, whole, left)
        copies += [far_right, far_left]
        far_right.wait_recv()
        last.append(passed(7, other, before, lower, right))
        far_left.wait_recv()
        last.append(passed(8, other, after, upper, left))
    for copy in last:
        copy.wait_recv()
    for copy in copies + last:
        copy.wait_send()
    own.wait()


def gathered(value, both, collective_id, name):
    blocks = (2, 4) if both else (4,)
    out = pl.pallas_call(
        functools.partial(gather_kernel, both),
        out_shape=jax.ShapeDtypeStruct((*blocks, *value.shape), value.dtype),
        in_specs=[pl.BlockSpec(memory_space=pl.ANY)],
        out_specs=pl.BlockSpec(memory_space=pl.ANY),
        scratch_shapes=[
            pltpu.SemaphoreType.DMA((9,)),
            pltpu.SemaphoreType.DMA((9,)),
            pltpu.SemaphoreType.DMA,
        ],
        compiler_params=pltpu.CompilerParams(collective_id=collective_id, has_side_effects=True),
        name=name,
    )(value)
    return out.reshape(-1, value.shape[-1])


def kernel_copies(send_sem, recv_sem):
    def sent(slot, source, goal, device):
        copy = pltpu.make_async_remote_copy(
            src_ref=source,
            dst_ref=goal,
            send_sem=send_sem.at[slot],
            recv_sem=recv_sem.at[slot],
            device_id=device,
            device_id_type=MESH,
        )
        copy.start()
        return copy

    return sent


def tensor_partner(step):
    goal = lax.rem(lax.axis_index("yh") * 4 + lax.axis_index("z") + step, 8)
    return {"yh": lax.div(goal, 4), "z": lax.rem(goal, 4)}


def spread(values):
    gap = jnp.zeros((values.shape[0], 16), values.dtype)
    return jnp.concatenate([values[:, :48], gap, values[:, 48:], gap], axis=1)


def packed(values):
    return jnp.concatenate([values[:, :48], values[:, 64:112]], axis=1)


def score_block(key_block, query_block, first_row, key_start, query_start):
    scores = times_transposed(key_block, query_block) * (HEAD_SIZE ** (-0.5))
    keys = key_start + lax.broadcasted_iota(jnp.int32, scores.shape, 0)
    queries = lax.broadcasted_iota(jnp.int32, (1, scores.shape[1]), 1)
    queries = query_start + jnp.where(queries >= 192, queries - 192, queries)
    return scores, (keys >= first_row) & (keys <= queries)


KEYS = 256


def key_blocks(block):
    return lax.div(3 * block + 6, 4)


def attend_kernel(
    normed_ref,
    weight_ref,
    cos_ref,
    sin_ref,
    first_ref,
    out_weight_ref,
    gate_up_ref,
    down_ref,
    cotangent_ref,
    normed_all_ref,
    out_all_ref,
    gate_up_other_ref,
    down_other_ref,
    near_ref,
    here_ref,
    q_ref,
    k_ref,
    v_ref,
    o_ref,
    lse_ref,
    landed,
    scores,
    outgoing,
    send_sem,
    recv_sem,
    local_sem,
):
    x, yl, c = lax.axis_index("x"), lax.axis_index("yl"), lax.axis_index("c")
    yh, z = lax.axis_index("yh"), lax.axis_index("z")
    me = yh * 4 + z
    after, before, opposite = lax.rem(z + 1, 4), lax.rem(z + 3, 4), lax.rem(z + 2, 4)
    other = 1 - yh
    right, left, across = {"z": after}, {"z": before}, {"yh": other}
    x_after, x_before, x_far = lax.rem(x + 1, 4), lax.rem(x + 3, 4), lax.rem(x + 2, 4)
    x_right, x_left, core = {"x": x_after}, {"x": x_before}, {"c": 1 - c}

    def crossed(step):
        place = tensor_partner(step)
        return {**place, "yl": lax.rem(yl + yh + place["yh"], 2)}

    tensor_partners = [tensor_partner(step) for step in range(1, 8)]
    cross_partners = [{"yl": 1 - yl, "yh": other, "z": lax.rem(z + k, 4)} for k in range(4)]
    barrier_with(tensor_partners + cross_partners + [x_right, x_left, core])
    sent = kernel_copies(send_sem, recv_sem)

    lower, upper, whole = pl.ds(0, 96), pl.ds(96, 96), pl.ds(0, 192)

    def shard(slot, block_yh, block_z, rows, device):
        place = landed.at[block_yh, block_z, rows]
        return sent(slot, place, place, device)

    def gate_up_part(ref, quarter, half, part=pl.ds(0, 2)):
        rows = pl.ds(pl.multiple_of(quarter * 384, 16), 384)
        return ref.at[part, rows, pl.ds(pl.multiple_of(half * 256, 128), 256)]

    def down_part(ref, quarter, half, part=pl.ds(0, 128)):
        rows = pl.ds(pl.multiple_of(quarter * 128 + part.start, 16), part.size)
        return ref.at[rows, pl.ds(pl.multiple_of(half * 768, 128), 768)]

    def out_part(ref, quarter, half, part=pl.ds(1, 7)):
        rows = pl.ds(pl.multiple_of(quarter * 48, 16), 48)
        return ref.at[part, rows, pl.ds(pl.multiple_of(half * 768, 128), 768)]

    copies, awaited = [], []

    def keep(copy):
        copies.append(copy)
        return copy

    def await_later(copy):
        awaited.append(copy)
        return keep(copy)

    to_right = keep(sent(0, normed_ref, landed.at[yh, z], right))
    to_left = keep(sent(1, normed_ref, landed.at[yh, z], left))
    to_across = keep(sent(2, normed_ref, landed.at[yh, z], across))
    own = pltpu.make_async_copy(normed_ref, landed.at[yh, z], local_sem.at[0])
    own.start()
    own_out = pltpu.make_async_copy(out_weight_ref, out_all_ref.at[0], local_sem.at[1])
    own_out.start()
    near_own = pltpu.make_async_copy(cotangent_ref, near_ref.at[z], local_sem.at[2])
    near_own.start()
    gate_up_cross = keep(
        sent(9, gate_up_part(gate_up_ref, x, c), gate_up_part(gate_up_other_ref, x, c), crossed(4))
    )
    down_cross = keep(
        sent(10, down_part(down_ref, x, c), down_part(down_other_ref, x, c), crossed(4))
    )
    out_cross = []
    piece = out_weight_ref.at[
        pl.ds(pl.multiple_of(x * 48, 16), 48), pl.ds(pl.multiple_of(c * 768, 128), 768)
    ]
    for step in range(1, 8):
        goal = out_all_ref.at[
            8 - step, pl.ds(pl.multiple_of(x * 48, 16), 48), pl.ds(pl.multiple_of(c * 768, 128), 768)
        ]
        out_cross.append(keep(sent(10 + step, piece, goal, crossed(step))))
    own.wait()

    def project(block_yh, block_z):
        block = block_yh * 4 + block_z
        projected = jnp.dot(
            landed[block_yh, block_z], weight_ref[...], preferred_element_type=jnp.float32
        )
        rows = pl.ds(pl.multiple_of(block * 192, 16), 192)
        cos_part, sin_part = cos_ref[rows, :], sin_ref[rows, :]

        def turned(values):
            return (values * cos_part + pltpu.roll(values, 64, 1) * sin_part).astype(jnp.bfloat16)

        q_ref[block, 0:192, :] = turned(projected[:, 0:128])
        q_ref[block, 192:384, :] = turned(projected[:, 128:256])
        k_ref[rows, :] = turned(projected[:, 256:384])
        v_ref[rows, :] = projected[:, 384:512].astype(jnp.bfloat16)

    project(yh, z)
    to_right.wait_recv()
    last_right = keep(shard(3, yh, before, lower, right))
    to_left.wait_recv()
    last_left = keep(shard(4, yh, after, upper, left))
    project(yh, before)
    project(yh, after)

    def spread_out(base, part, ref, halves):
        goal = part(ref, x, c)
        return [
            keep(sent(base, goal, goal, x_right)),
            keep(sent(base + 1, goal, goal, x_left)),
            await_later(sent(base + 4, goal, goal, core)),
        ]

    def pass_on(base, part, ref, halves, arriving):
        arriving[0].wait_recv()
        first, second = part(ref, x_before, c), part(ref, x_before, c, halves[0])
        far = [keep(sent(base + 2, second, second, x_right))]
        await_later(sent(base + 5, first, first, core))
        arriving[1].wait_recv()
        first, second = part(ref, x_after, c), part(ref, x_after, c, halves[1])
        far.append(keep(sent(base + 3, second, second, x_left)))
        await_later(sent(base + 6, first, first, core))
        return far

    def finish(base, part, ref, halves, far):
        for k in range(2):
            far[k].wait_recv()
            goal = part(ref, x_far, c, halves[k])
            await_later(sent(base + 7 + k, goal, goal, core))

    gate_up_plan = (18, gate_up_part, gate_up_other_ref, (pl.ds(0, 1), pl.ds(1, 1)))
    down_plan = (27, down_part, down_other_ref, (pl.ds(0, 64), pl.ds(64, 64)))
    out_plan = (36, out_part, out_all_ref, (pl.ds(1, 4), pl.ds(5, 3)))

    gate_up_cross.wait_recv()
    gate_up_moves = spread_out(*gate_up_plan)
    down_cross.wait_recv()
    down_moves = spread_out(*down_plan)
    to_across.wait_recv()
    far_right = keep(shard(5, other, z, whole, right))
    far_left = keep(shard(6, other, z, whole, left))
    for copy in out_cross:
        copy.wait_recv()
    out_moves = spread_out(*out_plan)
    last_right.wait_recv()
    last_left.wait_recv()
    project(other, z)
    project(yh, opposite)
    far_right.wait_recv()
    far_last_right = keep(shard(7, other, before, lower, right))
    far_left.wait_recv()
    far_last_left = keep(shard(8, other, after, upper, left))
    await_later(sent(45, cotangent_ref, near_ref.at[z], right))
    await_later(sent(46, cotangent_ref, near_ref.at[z], left))
    project(other, before)
    project(other, after)
    gate_up_far = pass_on(*gate_up_plan, gate_up_moves)
    down_far = pass_on(*down_plan, down_moves)
    far_last_right.wait_recv()
    far_last_left.wait_recv()
    project(other, opposite)
    stored = pltpu.make_async_copy(landed, normed_all_ref, local_sem.at[3])
    stored.start()

    def outgoing_copy(block, step):
        return pltpu.make_async_remote_copy(
            src_ref=outgoing.at[block],
            dst_ref=here_ref.at[lax.rem(8 - step, 8)],
            send_sem=send_sem.at[47 + step],
            recv_sem=recv_sem.at[47 + step],
            device_id={"yh": lax.div(block, 4), "z": lax.rem(block, 4)},
            device_id_type=MESH,
        )

    def attend(block, carry):
        query_block = q_ref[block]
        first_row = first_ref[block]
        count = key_blocks(block)

        def score(j, peak):
            rows = pl.ds(pl.multiple_of(j * KEYS, KEYS), KEYS)
            block_scores, allowed = score_block(
                k_ref[rows, :], query_block, first_row, j * KEYS, block * 192
            )
            block_scores = jnp.where(allowed, block_scores, masked_score)
            scores[rows, :] = block_scores
            return jnp.maximum(peak, jnp.max(block_scores.reshape(KEYS // 8, 8, 384), axis=0))

        peak = lax.fori_loop(0, count, score, jnp.full((8, 384), masked_score, jnp.float32))
        peak = jnp.max(peak, axis=0, keepdims=True)

        def weigh(j, state):
            total, out = state
            rows = pl.ds(pl.multiple_of(j * KEYS, KEYS), KEYS)
            weights = jnp.exp(scores[rows, :] - peak)
            total = total + jnp.sum(weights.reshape(KEYS // 8, 8, 384), axis=0)
            out = out + transposed_times(weights.astype(jnp.bfloat16), v_ref[rows, :])
            return total, out

        total, out = lax.fori_loop(
            0,
            count,
            weigh,
            (jnp.zeros((8, 384), jnp.float32), jnp.zeros((384, 128), jnp.float32)),
        )
        total = jnp.sum(total, axis=0, keepdims=True)
        lse_ref[block] = peak + jnp.log(total)
        out = out * jnp.transpose(jnp.broadcast_to(1.0 / total, (128, 384)))
        o_ref[block] = out.astype(jnp.bfloat16)
        outgoing[block] = jnp.concatenate([packed(out[0:192]), packed(out[192:384])], axis=1).astype(
            jnp.bfloat16
        )
        step = lax.rem(block - me + 8, 8)

        @pl.when(step != 0)
        def _():
            outgoing_copy(block, step).start()

        @pl.when(step == 0)
        def _():
            pltpu.make_async_copy(outgoing.at[block], here_ref.at[0], local_sem.at[4]).start()

        return carry

    lax.fori_loop(0, 8, attend, 0)
    out_far = pass_on(*out_plan, out_moves)
    finish(*gate_up_plan, gate_up_far)
    finish(*down_plan, down_far)
    finish(*out_plan, out_far)
    for copy in awaited:
        copy.wait_recv()
    for copy in copies:
        copy.wait_send()
    for step in range(1, 8):
        outgoing_copy(lax.rem(me + step, 8), step).wait()
    pltpu.make_async_copy(outgoing.at[me], here_ref.at[0], local_sem.at[4]).wait()
    own_out.wait()
    near_own.wait()
    stored.wait()


ANY = pl.BlockSpec(memory_space=pl.ANY)
IN_VMEM = pl.BlockSpec(memory_space=pltpu.VMEM)


def attended(normed, weight, cos_part, sin_part, first, out_weight, gate_up, down, cotangent):
    def shape(dims, kind=jnp.bfloat16):
        return jax.ShapeDtypeStruct(dims, kind)

    return pl.pallas_call(
        attend_kernel,
        out_shape=(
            shape((2, 4, 192, 1536)),
            shape((8, 192, 1536)),
            shape((2, 1536, 512)),
            shape((512, 1536)),
            shape((4, 192, 1536)),
            shape((8, 192, 192)),
            shape((8, 384, 128)),
            shape((1536, 128)),
            shape((1536, 128)),
            shape((8, 384, 128)),
            shape((8, 1, 384), jnp.float32),
        ),
        in_specs=[IN_VMEM] * 5 + [ANY] * 4,
        out_specs=(ANY,) * 6 + (IN_VMEM,) * 5,
        scratch_shapes=[
            pltpu.VMEM((2, 4, 192, 1536), jnp.bfloat16),
            pltpu.VMEM((1536, 384), jnp.float32),
            pltpu.VMEM((8, 192, 192), jnp.bfloat16),
            pltpu.SemaphoreType.DMA((55,)),
            pltpu.SemaphoreType.DMA((55,)),
            pltpu.SemaphoreType.DMA((5,)),
        ],
        compiler_params=pltpu.CompilerParams(
            collective_id=1, has_side_effects=True, vmem_limit_bytes=48 * 2**20
        ),
        name="attend",
    )(normed, weight, cos_part, sin_part, first, out_weight, gate_up, down, cotangent)


def branch_kernel(tokens_ref, here_ref, out_ref, gain_ref, middle_ref, normed_ref):
    middle = tokens_ref[...].astype(jnp.float32)
    for k in range(8):
        middle += jnp.dot(here_ref[k], out_ref[k], preferred_element_type=jnp.float32)
    middle_ref[...] = middle
    scale = lax.rsqrt(jnp.mean(middle * middle, axis=1, keepdims=True) + EPSILON)
    normed_ref[...] = (middle * scale * gain_ref[...]).astype(jnp.bfloat16)


def branched(tokens, here, out_all, gain):
    return pl.pallas_call(
        branch_kernel,
        out_shape=(
            jax.ShapeDtypeStruct(tokens.shape, jnp.float32),
            jax.ShapeDtypeStruct(tokens.shape, jnp.bfloat16),
        ),
        compiler_params=pltpu.CompilerParams(vmem_limit_bytes=48 * 2**20),
        name="branch",
    )(tokens, here, out_all, gain)


def attend_back_kernel(
    dn_ref,
    middle_ref,
    gain_ref,
    cotangent_ref,
    out_ref,
    here_ref,
    q_ref,
    k_ref,
    v_ref,
    o_ref,
    lse_ref,
    first_ref,
    cos_ref,
    sin_ref,
    dh_ref,
    out_grad_ref,
    dp_ref,
    outgoing,
    landed,
    dk_sum,
    dv_sum,
    low,
    send_sem,
    recv_sem,
):
    me = lax.axis_index("yh") * 4 + lax.axis_index("z")
    barrier_with([tensor_partner(step) for step in range(1, 8)])

    middle = middle_ref[...]
    scale = lax.rsqrt(jnp.mean(middle * middle, axis=1, keepdims=True) + EPSILON)
    unit = middle * scale
    scaled = dn_ref[...].astype(jnp.float32) * gain_ref[...]
    dh = cotangent_ref[...].astype(jnp.float32) + scale * (
        scaled - unit * jnp.mean(scaled * unit, axis=1, keepdims=True)
    )
    dh_ref[...] = dh
    low[...] = dh.astype(jnp.bfloat16)
    copies = []
    sent = kernel_copies(send_sem, recv_sem)
    for step in range(1, 8):
        outgoing[step] = times_transposed(low[...], out_ref[step]).astype(jnp.bfloat16)
        copies.append(
            sent(step, outgoing.at[step], landed.at[8 - step], tensor_partner(step))
        )
    landed[0] = times_transposed(low[...], out_ref[0]).astype(jnp.bfloat16)
    for k in range(8):
        out_grad_ref[k] = transposed_times(here_ref[k], low[...]).astype(jnp.bfloat16)
    dk_sum[...] = jnp.zeros_like(dk_sum)
    dv_sum[...] = jnp.zeros_like(dv_sum)

    def unturned(values, rows):
        return values * cos_ref[rows, :] - pltpu.roll(values, 64, 1) * sin_ref[rows, :]

    def back(step, carry):
        block = lax.rem(me + step, 8)

        @pl.when(step != 0)
        def _():
            pltpu.make_async_remote_copy(
                src_ref=outgoing.at[step],
                dst_ref=landed.at[step],
                send_sem=send_sem.at[step],
                recv_sem=recv_sem.at[8 - step],
                device_id=tensor_partner(1),
                device_id_type=MESH,
            ).wait_recv()

        arrived = landed[step]
        grad_block = jnp.concatenate(
            [spread(arrived[:, 0:96]), spread(arrived[:, 96:192])], axis=0
        )
        query_block = q_ref[block]
        first_row, lse = first_ref[block], lse_ref[block]
        centered = grad_block.astype(jnp.float32) * o_ref[block].astype(jnp.float32)
        centered = jnp.sum(jnp.transpose(centered), axis=0, keepdims=True)

        def key_step(j, dq):
            rows = pl.ds(pl.multiple_of(j * KEYS, KEYS), KEYS)
            key_block, value_block = k_ref[rows, :], v_ref[rows, :]
            block_scores, allowed = score_block(
                key_block, query_block, first_row, j * KEYS, block * 192
            )
            weights = jnp.where(allowed, jnp.exp(block_scores - lse), 0.0)
            grad_weights = times_transposed(value_block, grad_block)
            grad_scores = (weights * (grad_weights - centered)).astype(jnp.bfloat16)
            dv_sum[rows, :] += jnp.dot(
                weights.astype(jnp.bfloat16), grad_block, preferred_element_type=jnp.float32
            )
            dk_sum[rows, :] += jnp.dot(
                grad_scores, query_block, preferred_element_type=jnp.float32
            )
            return dq + transposed_times(grad_scores, key_block)

        dq = lax.fori_loop(
            0, key_blocks(block), key_step, jnp.zeros((384, 128), jnp.float32)
        ) * (HEAD_SIZE ** (-0.5))
        rows = pl.ds(pl.multiple_of(block * 192, 16), 192)
        dp_ref[rows, 0:128] = unturned(dq[0:192], rows).astype(jnp.bfloat16)
        dp_ref[rows, 128:256] = unturned(dq[192:384], rows).astype(jnp.bfloat16)
        return carry

    lax.fori_loop(0, 8, back, 0)

    def finish(block, carry):
        rows = pl.ds(pl.multiple_of(block * 192, 16), 192)
        dk = dk_sum[rows, :] * (HEAD_SIZE ** (-0.5))
        dp_ref[rows, 256:384] = unturned(dk, rows).astype(jnp.bfloat16)
        dp_ref[rows, 384:512] = dv_sum[rows, :].astype(jnp.bfloat16)
        return carry

    lax.fori_loop(0, 8, finish, 0)
    for copy in copies:
        copy.wait_send()


def attended_back(*arguments):
    return pl.pallas_call(
        attend_back_kernel,
        out_shape=(
            jax.ShapeDtypeStruct((192, 1536), jnp.float32),
            jax.ShapeDtypeStruct((8, 192, 1536), jnp.bfloat16),
            jax.ShapeDtypeStruct((1536, 512), jnp.bfloat16),
        ),
        scratch_shapes=[
            pltpu.VMEM((8, 192, 192), jnp.bfloat16),
            pltpu.VMEM((8, 192, 192), jnp.bfloat16),
            pltpu.VMEM((1536, 128), jnp.float32),
            pltpu.VMEM((1536, 128), jnp.float32),
            pltpu.VMEM((192, 1536), jnp.bfloat16),
            pltpu.SemaphoreType.DMA((8,)),
            pltpu.SemaphoreType.DMA((8,)),
        ],
        compiler_params=pltpu.CompilerParams(
            collective_id=2, has_side_effects=True, vmem_limit_bytes=56 * 2**20
        ),
        name="attend_back",
    )(*arguments)


def picked(value, index, dim):
    return lax.dynamic_index_in_dim(value, index, dim, keepdims=False)


def added(one, two):
    return (one.astype(jnp.float32) + two.astype(jnp.float32)).astype(jnp.bfloat16)


def summed_over_cores(grad):
    core = lax.axis_index("c")
    count, _, columns = grad.shape
    parts = grad.reshape(count, 4, 2, 2, 96, columns)

    def chosen(which):
        part = picked(parts, which, 3).reshape(count, 4, 192, columns)
        return jnp.transpose(part, (1, 0, 2, 3))

    arrived = to_other_core(chosen(1 - core))
    return added(chosen(core), arrived)


def summed_over_x(grad):
    _, count, _, columns = grad.shape
    out = lax.psum_scatter(grad, "x", scatter_dimension=0, tiled=True)
    return jnp.transpose(out.reshape(count, 2, 96, columns), (1, 0, 2, 3))


def summed_over_yl(grad):
    yl = lax.axis_index("yl")
    arrived = to_other_yl(picked(grad, 1 - yl, 0))
    return picked(grad, yl, 0).astype(jnp.float32) + arrived.astype(jnp.float32)


def summed_out_grad(grad):
    core, yl, yh = lax.axis_index("c"), lax.axis_index("yl"), lax.axis_index("yh")
    me = yh * 4 + lax.axis_index("z")
    halves = grad.reshape(8, 2, 96, 4, 384)

    def chosen(which):
        return jnp.transpose(picked(halves, which, 1), (2, 0, 1, 3))

    grad = added(chosen(core), to_other_core(chosen(1 - core)))
    grad = lax.psum_scatter(grad, "x", scatter_dimension=0, tiled=True).reshape(8, 96, 384)
    grad = lax.dynamic_slice_in_dim(jnp.concatenate([grad, grad], axis=0), 8 - me, 8, 0)
    grad = jnp.transpose(grad.reshape(2, 4, 96, 384), (1, 0, 2, 3))
    grad = lax.psum_scatter(grad, "z", scatter_dimension=0, tiled=True).reshape(2, 96, 384)
    grad = added(picked(grad, yh, 0), to_cross(picked(grad, 1 - yh, 0)))
    grad = jnp.transpose(grad.reshape(96, 2, 192), (1, 0, 2))
    grad = added(picked(grad, yl, 0), to_other_yl(picked(grad, 1 - yl, 0)))
    grad = jnp.transpose(grad.reshape(96, 2, 96), (1, 0, 2))
    mine, theirs = picked(grad, core, 0), to_other_core(picked(grad, 1 - core, 0))
    in_order = core == 0
    return jnp.concatenate(
        [jnp.where(in_order, mine, theirs), jnp.where(in_order, theirs, mine)], axis=0
    ).astype(jnp.float32)


def per_device(
    tokens,
    seq_lens,
    query_key_value_weight,
    out_weight,
    gate_up_weight,
    down_weight,
    norm_gains,
    cotangent,
):
    shard_rows = tokens.shape[0]
    group_rows = shard_rows * 8
    core, yh = lax.axis_index("c"), lax.axis_index("yh")
    me = yh * 4 + lax.axis_index("z")

    hidden = tokens.astype(jnp.float32)
    unit_one, scale_one = normalize(hidden)
    normed = (unit_one * norm_gains[0]).astype(jnp.bfloat16)
    first, positions = layout(seq_lens[0], group_rows)
    cos_part, sin_part = angles(positions)
    gap = jnp.zeros((group_rows, 16), jnp.float32)
    cos_part = jnp.concatenate([cos_part, gap, cos_part, gap], axis=1)
    sin_part = jnp.concatenate([-sin_part, gap, sin_part, gap], axis=1)
    first = jnp.tile(first.reshape(8, 1, shard_rows), (1, 1, 2))
    weight_wide = spread_columns(query_key_value_weight)
    (
        normed_all,
        out_all,
        gate_up_other,
        down_other,
        upstream_near,
        attended_here,
        queries,
        keys_all,
        values_all,
        heads,
        log_sums,
    ) = attended(
        normed,
        weight_wide,
        cos_part,
        sin_part,
        first,
        out_weight,
        gate_up_weight,
        down_weight,
        cotangent,
    )
    normed_all = normed_all.reshape(group_rows, -1)

    middle, normed_two = branched(tokens, attended_here, out_all, norm_gains[1:2])
    normed_two_all = gathered(normed_two, False, 3, "gather_normed_two")
    upstream_all = gathered(cotangent, False, 4, "gather_upstream")
    gate_up_all = jnp.concatenate([gate_up_weight, gate_up_other], axis=2)
    down_all = jnp.concatenate([down_weight, down_other], axis=0)
    gate_up = jnp.einsum(
        "td,cdf->ctf", normed_two_all, gate_up_all, preferred_element_type=jnp.float32
    )
    sigmoid_gate = jax.nn.sigmoid(gate_up[0])
    silu_gate = gate_up[0] * sigmoid_gate
    activated = (silu_gate * gate_up[1]).astype(jnp.bfloat16)
    grad_act = times_transposed(upstream_all, down_all)
    grad_gate = grad_act * gate_up[1] * sigmoid_gate * (1.0 + gate_up[0] * (1.0 - sigmoid_gate))
    grad_upper = grad_act * silu_gate
    grad_gate_up = jnp.stack([grad_gate, grad_upper]).astype(jnp.bfloat16)
    normed_two_part = jnp.einsum(
        "ctf,cdf->td", grad_gate_up, gate_up_all, preferred_element_type=jnp.float32
    ).astype(jnp.bfloat16)
    grad_normed_two = lax.psum_scatter(normed_two_part, "z", scatter_dimension=0, tiled=True)
    activated, normed_two_all, upstream_all, normed_two_part = lax.optimization_barrier(
        (activated, normed_two_all, upstream_all, normed_two_part)
    )
    ffn_out = lax.psum_scatter(
        jnp.dot(activated, down_all, preferred_element_type=jnp.float32).astype(jnp.bfloat16),
        "z",
        scatter_dimension=0,
        tiled=True,
    ).astype(jnp.float32)
    mixed = (middle + ffn_out).astype(jnp.bfloat16)
    down_grad = transposed_times(upstream_all, activated).astype(jnp.bfloat16)
    gate_up_grad = jnp.einsum(
        "td,ctf->cdf", normed_two_all, grad_gate_up, preferred_element_type=jnp.float32
    ).astype(jnp.bfloat16)
    ffn_grad = jnp.concatenate([gate_up_grad, down_grad[None]], axis=0)

    grad_middle, out_grad, grad_projected = attended_back(
        grad_normed_two,
        middle,
        norm_gains[1:2],
        cotangent,
        out_all,
        attended_here,
        queries,
        keys_all,
        values_all,
        heads,
        log_sums,
        first,
        cos_part,
        sin_part,
    )
    by_z = jnp.transpose(
        grad_projected.reshape(2, 4, shard_rows, 512), (1, 0, 2, 3)
    ).reshape(group_rows, 512)
    normed_part = times_transposed(by_z, weight_wide).astype(jnp.bfloat16)
    grad_normed = lax.psum_scatter(normed_part, "z", scatter_dimension=0, tiled=True)
    grad_normed = lax.psum_scatter(grad_normed, "yh", scatter_dimension=0, tiled=True).astype(
        jnp.float32
    )
    grad_projected, normed_all, normed_part = lax.optimization_barrier(
        (grad_projected, normed_all, normed_part)
    )
    qkv_grad = transposed_times(normed_all, grad_projected).astype(jnp.bfloat16)
    qkv_grad = packed_columns(qkv_grad)
    input_grad = grad_middle + norm_back(grad_normed, unit_one, scale_one, norm_gains[0])

    ffn_grad = summed_over_x(summed_over_cores(ffn_grad))
    ffn_grad = (
        ffn_grad[..., :512].astype(jnp.float32) + to_cross(ffn_grad[..., 512:]).astype(jnp.float32)
    ).astype(jnp.bfloat16)
    ffn_grad = summed_over_yl(ffn_grad)
    qkv_grad = summed_over_yl(summed_over_x(summed_over_cores(qkv_grad[None])))[0]
    out_grad = summed_out_grad(out_grad)

    first = ((lax.axis_index("x") * 2 + lax.axis_index("yl")) * 2 + core) * 96
    rows_one = lax.dynamic_slice_in_dim(query_key_value_weight, first, 96, 0).astype(jnp.float32)
    rows_two = lax.dynamic_slice_in_dim(gate_up_weight, first, 96, 1).astype(jnp.float32)
    gain_rows = lax.dynamic_slice_in_dim(norm_gains, first, 96, 1)
    gains_grad = jnp.stack(
        [
            jnp.sum(qkv_grad * rows_one, axis=1),
            jnp.sum(ffn_grad[0:2] * rows_two, axis=(0, 2)),
        ]
    )
    copies = jnp.broadcast_to(gains_grad, (8, *gains_grad.shape))
    copies = lax.all_to_all(copies, TENSOR, split_axis=0, concat_axis=0, tiled=True)
    gains_grad = jnp.sum(copies, axis=0) / gain_rows
    return (
        mixed,
        input_grad,
        qkv_grad,
        out_grad,
        ffn_grad[0:2],
        ffn_grad[2].T,
        gains_grad,
    )


def solution(mesh):
    split = Mesh(mesh.devices.reshape(4, 2, 2, 2, 4), ALL)
    placed = (
        P(ALL, None),
        P(DP, None),
        P(None, TENSOR),
        P(TENSOR, None),
        P(None, None, TENSOR),
        P(TENSOR, None),
        P(),
        P(ALL, None),
    )
    return jax.shard_map(
        per_device,
        mesh=split,
        in_specs=placed,
        out_specs=(
            P(ALL, None),
            P(ALL, None),
            P(DP, TENSOR),
            P(TENSOR, DP),
            P(None, DP, TENSOR),
            P(TENSOR, DP),
            P(None, DP),
        ),
        check_vma=False,
    )
```

time: 665 us -> 544 us (0.82)
  waiting for transfers between devices: 264 us -> 158 us
  Pallas kernels: 108 us -> 185 us
  matrix products: 114 us -> 45.1 us
  other arithmetic: 67.7 us -> 41.9 us
  starting transfers between devices: 27.9 us -> 14.5 us
  local copies, waits for them, and re-layouts: 62.1 us -> 72.7 us
    pallas_call x2 -> x3, Pallas kernels: 27.9 us -> 137 us  [the longest x1 92 us: attended(): pl.pallas_call(attend_kernel, out_shape=(shape((2, 4, 192, 1536)), shape(...]
    unnamed x12 -> x10, waiting for transfers between devices: 66 us -> 0.83 us
    all_gather x3 -> x0, waiting for transfers between devices: 61.1 us -> none  [the longest x1 61.1 us: per_device(): out_halves = lax.all_gather(out_half, TENSOR, axis=0, tiled=True)]
    dot_general x20 -> x0, matrix products: 51.5 us -> none  [the longest x3 17.8 us: per_device(): jnp.einsum('qjd,kd->jqk', grad_block, values_all, preferred_element_type=...]
    pallas_call x2, Pallas kernels: 79.8 us -> 48.3 us  [gathered(): pl.pallas_call(functools.partial(gather_kernel, both), out_shape=jax.Shap...]
    reduce_scatter x1, waiting for transfers between devices: 0.01 us -> 14.2 us  [per_device(): lax.psum_scatter(normed_two_part, 'z', scatter_dimension=0, tiled=True)]
    reduce_scatter x1, waiting for transfers between devices: 18.6 us -> 4.76 us  [per_device(): lax.psum_scatter(grad_normed, 'yh', scatter_dimension=0, tiled=True)]
    convert_element_type x9 -> x7, other arithmetic: 30.5 us -> 17.6 us  [the longest x5 14.9 us: added(): (one.astype(jnp.float32) + two.astype(jnp.float32)).astype(jnp.bfloat16)]
  transfers between devices with their start and end apart: 24 -> 18, of which waited for: 11 -> 9; matrix products, arithmetic and copies ran while one was open for 33% -> 15% of each run, Pallas kernels for 16% -> 7%
where the time goes in v2:
time: 544 us; the launch traced here: 534 us
  Pallas kernels  185 us (34%)
  waiting for transfers between devices  158 us (29%)
  local copies, waits for them, and re-layouts  72.7 us (13%)
  matrix products  45.1 us (8%)
  other arithmetic  41.9 us (8%)
  between operations  17 us (3%)
  starting transfers between devices  14.5 us (3%)
    pallas_call x1, Pallas kernels, attended(): pl.pallas_call(attend_kernel, out_shape=(shape((2, 4, 192, 1536)), shape(...  92 us
    reduce_scatter x1, waiting for transfers between devices, per_device(): lax.psum_scatter(normed_part, 'z', scatter_dimension=0, tiled=True)  51.3 us
    pallas_call x2, Pallas kernels, gathered(): pl.pallas_call(functools.partial(gather_kernel, both), out_shape=jax.Shap...  48.3 us
    pallas_call x1, Pallas kernels, attended_back(): pl.pallas_call(attend_back_kernel, out_shape=(jax.ShapeDtypeStruct((192,...  39.9 us
    reduce_scatter x1, waiting for transfers between devices, per_device(): lax.psum_scatter(jnp.dot(activated, down_all, preferred_element_type=jnp....  34.7 us
    reduce_scatter x1, waiting for transfers between devices, summed_out_grad(): lax.psum_scatter(grad, 'x', scatter_dimension=0, tiled=True)  28.6 us
    unnamed x82, local copies, waits for them, and re-layouts  23.7 us
    dynamic_slice x4, local copies, waits for them, and re-layouts, picked(): return lax.dynamic_index_in_dim(value, index, dim, keepdims=False)  16.9 us
  transfers between devices with their start and end apart: 18, of which 9 were waited for; matrix products, arithmetic and copies ran while one was open for 15% of the time, Pallas kernels for 7%

profile of v2, /device:TPU:1, one launch (start us, length us, event | category | flops | bytes accessed | tf_op | source)
XLA Modules:
  0.0 534.3 jit_solution(17854231516340102059)
XLA Ops:
  10.7 1.3 fusion.22
  12.0 1.6 copy.101
  13.7 1.6 copy.102.weight_ref
  15.5 4.0 constant_dynamic-update-slice_fusion.1
  19.5 1.3 constant_dynamic-update-slice_fusion.3
  20.8 25.4 %gather_upstream.1 = bf16[4,192,1536]{2,1,0:T(8,128)(2,1)} custom-call(bf16[192,1536]{1,0:T(8,128)(2,1)} %cotangent_ref.3), custom_call_target="tpu_custom_call" | custom-call | tf_op jit(solution)/shard_map/gather_upstream/pallas_call | solution.py:166
  46.4 2.8 fusion.27
  49.3 1.8 pad_maximum_fusion.3
  51.1 92.0 %attend.1 = (bf16[2,4,192,1536]{3,2,1,0:T(8,128)(2,1)}, bf16[8,192,1536]{2,1,0:T(8,128)(2,1)}, bf16[2,1536,512]{2,1,0:T(8,128)(2,1)}, bf16[512,1536]{1,0:T(8,128...) custom-call(bf16[192,1536]{1,0:T(8,128)(2,1)S(1)} %fusion.17.normed_, ...), custom_call_target="tpu_custom_call" | custom-call | tf_op jit(solution)/shard_map/attend/pallas_call | solution.py:495
  145.2 4.7 branch.1
  150.0 1.0 copy-done.3
  151.8 23.0 %gather_normed_two.1 = bf16[4,192,1536]{2,1,0:T(8,128)(2,1)} custom-call(bf16[192,1536]{1,0:T(8,128)(2,1)} %copy-done.9), custom_call_target="tpu_custom_call" | custom-call | tf_op jit(solution)/shard_map/gather_normed_two/pallas_call | solution.py:166
  174.8 4.0 constant_dynamic-update-slice_fusion
  178.8 7.6 %convolution_bitcast_fusion = f32[2,768,1024]{1,2,0:T(8,128)S(1)} fusion(bf16[2,1536,1024]{2,1,0:T(8,128)(2,1)} %constant_dynamic-update-slice_fusion, bf16[768,1536,1]{1,0,2:T(8,128)(2,1)S(1)} %bitcast.186), kind=kOutput, calls=%fused_computation.30 | convolution fusion | flops 4831838208 | bytes 14942208 | tf_op jit(solution)/shard_map/td,cdf->ctf/dot_general | solution.py:800
  186.5 2.6 copy-done.20
  189.2 4.6 fusion.13
  193.8 1.2 copy-done.31
  195.4 6.5 %bitcast_convert_fusion = bf16[768,1536]{1,0:T(8,128)(2,1)} fusion(bf16[2,1536,1024]{2,1,0:T(8,128)(2,1)S(1)} %bitcast.189, bf16[1,768,1024]{1,2,0:T(8,128)(2,1)S(1)} %get-tuple-element.54, bf16[1,768,1024]{1,2,0:T(8,128)(2,1)S(1)} %get-tuple-element.53), kind=kOutput, calls=%fused_computation.14 | convolution fusion | flops 4834590720 | bytes 11796480 | tf_op jit(solution)/shard_map/ctf,cdf->td/dot_general | solution.py:810
  201.9 9.1 %convert_bitcast_fusion.1 = bf16[2,1536,1024]{1,2,0:T(8,128)(2,1)} fusion(bf16[768,1536]{1,0:T(8,128)(2,1)} %bitcast.185, bf16[1,768,1024]{1,2,0:T(8,128)(2,1)} %copy-done.32, bf16[1,768,1024]{1,2,0:T(8,128)(2,1)} %copy-done.31), kind=kOutput, calls=%fused_computation.8 | convolution fusion | flops 4836556800 | bytes 11796480 | tf_op jit(solution)/shard_map/td,ctf->cdf/dot_general | solution.py:825
  211.1 8.7 %copy.114 = bf16[2,1536,1024]{2,1,0:T(8,128)(2,1)} copy(bf16[2,1536,1024]{1,2,0:T(8,128)(2,1)} %convert_bitcast_fusion.1) | data formatting | bytes 12582912 | tf_op jit(solution)/shard_map/convert_element_type | solution.py:827
  219.7 4.5 convolution_convert_fusion.1
  224.2 4.0 fusion.3
  228.2 1.4 collective-permute-start.6
  230.1 7.4 %collective-permute-done.6 = bf16[4,3,192,1024]{3,2,0,1:T(8,128)(2,1)} collective-permute-done((bf16[4,3,192,1024]{3,2,0,1:T(8,128)(2,1)}, bf16[4,3,192,1024]{3,2,0,1:T(8,128)(2,1)}, u32[]{:S(2)}, u32[]{:S(2)}) %collective-permute-start.6) | collective-permute-done | bytes 4718624 | tf_op jit(solution)/shard_map/ppermute | solution.py:86
  237.5 8.4 %fusion.1 = bf16[4,3,192,1024]{3,2,0,1:T(8,128)(2,1)} fusion(bf16[4,3,192,1024]{3,2,0,1:T(8,128)(2,1)} %collective-permute-done.6, bf16[3,4,2,1,96,1024]{5,4,3,2,1,0:T(8,128)(2,1)} %get-tuple-element.51), kind=kLoop, calls=%fused_computation.6 | loop fusion | flops 9437184 | bytes 14155776 | tf_op jit(solution)/shard_map/convert_element_type | solution.py:693
  245.9 14.2 %reduce-scatter.15.cloned.1.call-done.dn_ref = bf16[192,1536]{1,0:T(8,128)(2,1)} async-done(((bf16[768,1536]{1,0:T(8,128)(2,1)}), bf16[192,1536]{1,0:T(8,128)(2,1)}) %reduce-scatter.15.cloned.1.call-update) | async-done | bytes 589840 | tf_op jit(solution)/shard_map/reduce_scatter | solution.py:813
  260.1 39.9 %attend_back.1 = (f32[192,1536]{1,0:T(8,128)}, bf16[8,192,1536]{2,1,0:T(8,128)(2,1)}, bf16[1536,512]{1,0:T(8,128)(2,1)}) custom-call(bf16[192,1536]{1,0:T(8,128)(2,1)} %reduce-scatter.15.cloned.1.call-done.dn_ref, f32[192,1536]{1,0:T(8,128)} %copy-done.3, f32[1,1536]{1,0:T(1,128)} %copy-done.13, bf16[192,1536]{1,0:T(8,128)(2,1)} %cotangent_ref.3, ...), custom_call_target="tpu_custom_call" | custom-call | tf_op jit(solution)/shard_map/attend_back/pallas_call | solution.py:665
  300.1 1.6 copy.105
  301.9 4.4 convolution_convert_fusion
  306.3 9.2 %reshape.217 = bf16[8,2,96,4,384]{4,3,2,1,0:T(4,128)(2,1)} reshape(bf16[8,192,1536]{2,1,0:T(8,128)(2,1)} %get-tuple-element.44) | data formatting | bytes 9437184 | tf_op jit(solution)/shard_map/reshape | solution.py:724
  315.5 5.5 %constant_dynamic-slice_fusion.5 = (bf16[8,1,96,4,384]{4,3,2,1,0:T(4,128)(2,1)}, bf16[8,1,96,4,384]{4,3,2,1,0:T(4,128)(2,1)S(1)}) fusion(bf16[8,2,96,4,384]{4,3,2,1,0:T(4,128)(2,1)} %reshape.217, s32[]{:T(128)S(6)} %select_n.84, s32[]{:T(128)S(6)} %select_n.85), kind=kLoop, calls=%fused_computation.99 | loop fusion | bytes 9437192 | tf_op jit(solution)/shard_map/jit(dynamic_index_in_dim)/dynamic_slice | solution.py:689
  321.0 1.8 copy.133
  322.8 1.5 collective-permute-start.2
  324.4 2.7 convolution_convert_fusion.3
  327.2 1.4 reshape_broadcast_in_dim_reshape.3
  328.5 5.0 constant_dynamic-slice_fusion.7
  333.5 4.6 copy.107
  338.2 3.7 copy.125
  341.9 2.0 fusion.23
  344.0 3.6 fusion.5
  347.7 1.3 copy-done.30
  349.0 5.7 %convolution_convert_fusion.2 = bf16[768,1536]{1,0:T(8,128)(2,1)} fusion(bf16[768,1024]{0,1:T(8,128)(2,1)S(1)} %copy-done.30, bf16[1024,1536]{1,0:T(8,128)(2,1)} %copy-done.26), kind=kOutput, calls=%fused_computation.16 | convolution fusion | flops 2417098752 | bytes 7077888 | tf_op jit(solution)/shard_map/dot_general | solution.py:818
  356.2 2.1 constant_dynamic-slice_fusion.8
  359.7 9.1 %reduce-scatter.21.cloned.1.call-done = bf16[1,1,192,384]{3,2,0,1:T(8,128)(2,1)} async-done(((bf16[4,1,192,384]{3,2,0,1:T(8,128)(2,1)}), bf16[1,1,192,384]{3,2,0,1:T(8,128)(2,1)}) %reduce-scatter.21.cloned.1.call-update) | async-done | bytes 147472 | tf_op jit(solution)/shard_map/reduce_scatter | solution.py:711
  368.8 1.5 dynamic-slice_bitcast_fusion.3
  371.3 2.8 collective-permute-done.7
  374.1 1.3 add_convert_fusion
  375.3 28.6 %reduce-scatter.23.cloned.1.call-done = bf16[1,8,96,384]{3,2,1,0:T(8,128)(2,1)} async-done(((bf16[4,8,96,384]{3,2,1,0:T(8,128)(2,1)}), bf16[1,8,96,384]{3,2,1,0:T(8,128)(2,1)}) %reduce-scatter.23.cloned.1.call-update) | async-done | bytes 589840 | tf_op jit(solution)/shard_map/reduce_scatter | solution.py:730
  404.0 2.1 fusion.26
  406.2 1.3 collective-permute-start.8
  407.5 34.7 %reduce-scatter.13.cloned.1.call-done = bf16[192,1536]{1,0:T(8,128)(2,1)} async-done(((bf16[768,1536]{1,0:T(8,128)(2,1)}), bf16[192,1536]{1,0:T(8,128)(2,1)}) %reduce-scatter.13.cloned.1.call-update) | async-done | bytes 589840 | tf_op jit(solution)/shard_map/reduce_scatter | solution.py:817
  442.2 2.0 add_convert_fusion.1
  444.2 51.3 %reduce-scatter.17.cloned.1.call-done = bf16[384,1536]{1,0:T(8,128)(2,1)} async-done(((bf16[1536,1536]{1,0:T(8,128)(2,1)}), bf16[384,1536]{1,0:T(8,128)(2,1)}) %reduce-scatter.17.cloned.1.call-update) | async-done | bytes 1179664 | tf_op jit(solution)/shard_map/reduce_scatter | solution.py:850
  495.6 1.7 multiply_reduce_fusion.1
  497.4 1.9 multiply_reduce_fusion
  500.3 2.5 collective-permute-start.3
  503.3 3.3 all-to-all-start
  506.7 0.9 fusion.28
  508.7 4.4 all-to-all-done
  513.4 2.7 collective-permute-start.5
  516.1 1.3 fusion.32
  518.2 4.8 reduce-scatter.19.cloned.1.call-done
  523.0 1.4 fusion.18
  524.4 2.4 fusion.21
  (141 shorter events, 14.7 us)
Async XLA Ops:
  8.0 252.1 %reduce-scatter.15.cloned.1.call-start = ((), (), s32[]{:S(2)}) async-start(), calls=%async_computation.8 | async-start | bytes 2949120 | tf_op jit(solution)/shard_map/reduce_scatter | solution.py:813
  10.7 134.5 %copy-start.13 = (f32[1,1536]{1,0:T(1,128)}, f32[1,1536]{1,0:T(1,128)S(1)}, u32[]{:S(2)}) copy-start(f32[1,1536]{1,0:T(1,128)S(1)} %get-tuple-element.68.gain_ref) | copy-start | bytes 18436
  13.7 1.7 copy-start.18
  15.5 35.6 %copy-start.12 = (s32[8,1,384]{2,1,0:T(1,128)}, s32[8,1,384]{2,1,0:T(1,128)S(1)}, u32[]{:S(2)}) copy-start(s32[8,1,384]{2,1,0:T(1,128)S(1)} %tile.9.first_ref) | copy-start | bytes 36868
  15.5 4.0 copy-start.17
  19.5 26.7 %copy-start = (bf16[192,1536]{1,0:T(8,128)(2,1)S(1)}, bf16[192,1536]{1,0:T(8,128)(2,1)}, u32[]{:S(2)}) copy-start(bf16[192,1536]{1,0:T(8,128)(2,1)} %tokens_ref.1) | copy-start | bytes 1769476
  49.3 1.8 copy-start.2
  49.3 1.8 copy-start.8
  51.1 92.0 %copy-start.1 = (f32[1536,128]{1,0:T(8,128)}, f32[1536,128]{1,0:T(8,128)S(1)}, u32[]{:S(2)}) copy-start(f32[1536,128]{1,0:T(8,128)S(1)} %get-tuple-element.61.cos_ref) | copy-start | bytes 2359300
  143.1 0.7 copy-start.10
  143.8 0.8 copy-start.11
  144.6 0.6 copy-start.14
  145.2 4.7 copy-start.5
  145.2 4.7 copy-start.6
  145.2 4.8 copy-start.7
  149.9 1.0 copy-start.3
  151.0 0.8 copy-start.9
  174.8 4.0 copy-start.21
  178.8 7.6 %copy-start.23 = (bf16[512,1536]{1,0:T(8,128)(2,1)S(1)}, bf16[512,1536]{1,0:T(8,128)(2,1)}, u32[]{:S(2)}) copy-start(bf16[512,1536]{1,0:T(8,128)(2,1)} %get-tuple-element.32) | copy-start | bytes 4718596
  178.8 7.6 %copy-start.25 = (bf16[1024,1536]{1,0:T(8,128)(2,1)S(1)}, bf16[1024,1536]{1,0:T(8,128)(2,1)}, u32[]{:S(2)}) copy-start(bf16[1024,1536]{1,0:T(8,128)(2,1)} %constant_dynamic-update-slice_fusion.3) | copy-start | bytes 9437188
  186.4 2.8 copy-start.20
  186.4 9.0 %slice-start = ((s8[6291456]{0:T(1024)(128)(4,1)}), s8[4194304]{0:T(1024)(128)(4,1)S(1)}, s32[]{:S(2)}) async-start(s8[6291456]{0:T(1024)(128)(4,1)} %bitcast.188), calls=%async_computation.15 | async-start | bytes 8388608
  186.5 7.2 %copy-start.26 = (bf16[1024,1536]{1,0:T(8,128)(2,1)}, bf16[1024,1536]{1,0:T(8,128)(2,1)S(1)}, u32[]{:S(2)}) copy-start(bf16[1024,1536]{1,0:T(8,128)(2,1)S(1)} %constant_dynamic-update-slice_fusion.2) | copy-start | bytes 9437188
  189.2 6.3 %slice-start.1 = ((s8[6291456]{0:T(1024)(128)(4,1)}), s8[2097152]{0:T(1024)(128)(4,1)S(1)}, s32[]{:S(2)}) async-start(s8[6291456]{0:T(1024)(128)(4,1)} %bitcast.188), calls=%async_computation.16 | async-start | bytes 4194304
  193.8 1.2 copy-start.31
  193.8 1.6 copy-start.32
  219.7 4.5 copy-start.15
  228.2 9.3 %collective-permute-start.6 = (bf16[4,3,192,1024]{3,2,0,1:T(8,128)(2,1)}, bf16[4,3,192,1024]{3,2,0,1:T(8,128)(2,1)}, u32[]{:S(2)}, u32[]{:S(2)}) collective-permute-start(bf16[4,3,192,1024]{3,2,0,1:T(8,128)(2,1)} %bitcast.45), channel_id=1, source_target_pairs={{0,8},{8,0},{1,9},{9,1},{2,10},{10,2},{3,11},{11,3},{4,12},{12,4},... | collective-permute-start | bytes 14155784 | tf_op jit(solution)/shard_map/ppermute | solution.py:86
  229.6 126.6 %all-reduce.8.cloned.1.call-start = ((), (), s32[]{:S(2)}) async-start(), calls=%async_computation.14 | async-start | bytes 9437184
  245.9 123.0 %reduce-scatter.21.cloned.1.call-start = ((), (), s32[]{:S(2)}) async-start(), calls=%async_computation.11 | async-start | bytes 737280 | tf_op jit(solution)/shard_map/reduce_scatter | solution.py:711
  300.1 1.9 copy-start.19
  306.3 18.1 %slice-start.2 = ((s8[4718592]{0:T(1024)(128)(4,1)}), s8[524288]{0:T(1024)(128)(4,1)S(1)}, s32[]{:S(2)}) async-start(s8[4718592]{0:T(1024)(128)(4,1)} %bitcast.201), calls=%async_computation.17 | async-start | bytes 1048576
  315.5 8.9 %slice-start.3 = ((s8[4718592]{0:T(1024)(128)(4,1)}), s8[4194304]{0:T(1024)(128)(4,1)S(1)}, s32[]{:S(2)}) async-start(s8[4718592]{0:T(1024)(128)(4,1)} %bitcast.201), calls=%async_computation.18 | async-start | bytes 8388608
  321.0 3.4 copy-start.22
  322.8 21.2 %collective-permute-start.2 = (bf16[4,8,96,384]{3,2,1,0:T(8,128)(2,1)}, bf16[4,8,96,384]{3,2,1,0:T(8,128)(2,1)}, u32[]{:S(2)}, u32[]{:S(2)}) collective-permute-start(bf16[4,8,96,384]{3,2,1,0:T(8,128)(2,1)} %bitcast.174), channel_id=1, source_target_pairs={{0,8},{8,0},{1,9},{9,1},{2,10},{10,2},{3,11},{11,3},{4,12},{12,4},... | collective-permute-start | bytes 7077896 | tf_op jit(solution)/shard_map/ppermute | solution.py:86
  338.1 5.8 %copy-start.16 = (bf16[8,1,96,4,384]{4,3,2,1,0:T(4,128)(2,1)S(1)}, bf16[8,1,96,4,384]{4,3,2,1,0:T(4,128)(2,1)}, u32[]{:S(2)}) copy-start(bf16[8,1,96,4,384]{4,3,2,1,0:T(4,128)(2,1)} %get-tuple-element.56) | copy-start | bytes 7077892
  338.1 3.7 collective-permute-start
  343.9 60.1 %reduce-scatter.23.cloned.1.call-start = ((), (), s32[]{:S(2)}) async-start(), calls=%async_computation.12 | async-start | bytes 2949120 | tf_op jit(solution)/shard_map/reduce_scatter | solution.py:730
  347.6 1.4 copy-start.30
  347.6 94.6 %reduce-scatter.13.cloned.1.call-start = ((), (), s32[]{:S(2)}) async-start(), calls=%async_computation.7 | async-start | bytes 2949120 | tf_op jit(solution)/shard_map/reduce_scatter | solution.py:817
  354.8 0.8 copy-start.29
  354.8 140.7 %reduce-scatter.17.cloned.1.call-start = ((), (), s32[]{:S(2)}) async-start(), calls=%async_computation.9 | async-start | bytes 5898240 | tf_op jit(solution)/shard_map/reduce_scatter | solution.py:850
  355.5 2.9 copy-start.28
  355.5 143.8 %all-reduce.6.cloned.1.call-start = ((), (), s32[]{:S(2)}) async-start(), calls=%async_computation.13 | async-start | bytes 1179648
  358.3 83.9 %copy-start.4 = (f32[192,1536]{1,0:T(8,128)S(1)}, f32[192,1536]{1,0:T(8,128)}, u32[]{:S(2)}) copy-start(f32[192,1536]{1,0:T(8,128)} %copy-done.3) | copy-start | bytes 3538948
  358.3 15.7 %collective-permute-start.7 = (bf16[2,3,96,512]{3,2,0,1:T(8,128)(2,1)S(1)}, bf16[2,3,96,512]{3,2,0,1:T(8,128)(2,1)}, u32[]{:S(2)}, u32[]{:S(2)}) collective-permute-start(bf16[2,3,96,512]{3,2,0,1:T(8,128)(2,1)S(1)} %slice.46), channel_id=1, source_target_pairs={{0,20},{4,16},{16,4},{20,0},{1,21},{5,17},{17,5},{21,1},{2,22},{6,... | collective-permute-start | bytes 1769480 | tf_op jit(solution)/shard_map/ppermute | solution.py:92
  370.4 125.2 %collective-permute-start.1 = (bf16[1,96,384]{2,1,0:T(8,128)(2,1)}, bf16[1,96,384]{2,1,0:T(8,128)(2,1)}, u32[]{:S(2)}, u32[]{:S(2)}) collective-permute-start(bf16[1,96,384]{2,1,0:T(8,128)(2,1)} %dynamic-slice_bitcast_fusion.3), channel_id=1, source_target_pairs={{0,16},{16,0},{1,17},{17,1},{2,18},{18,2},{3,19},{19,3},{4,20},{20... | collective-permute-start | bytes 221192 | tf_op jit(solution)/shard_map/ppermute | solution.py:96
  406.1 89.4 %copy-start.27 = (bf16[1,1,192,384]{3,2,0,1:T(8,128)(2,1)S(1)}, bf16[1,1,192,384]{3,2,0,1:T(8,128)(2,1)}, u32[]{:S(2)}) copy-start(bf16[1,1,192,384]{3,2,0,1:T(8,128)(2,1)} %reduce-scatter.21.cloned.1.call-done) | copy-start | bytes 442372
  406.1 116.8 %reduce-scatter.19.cloned.1.call-start = ((), (), s32[]{:S(2)}) async-start(), calls=%async_computation.10 | async-start | bytes 1769472 | tf_op jit(solution)/shard_map/reduce_scatter | solution.py:851
  406.2 91.1 %collective-permute-start.8 = (bf16[3,96,512]{2,1,0:T(8,128)(2,1)S(1)}, bf16[3,96,512]{2,1,0:T(8,128)(2,1)S(1)}, u32[]{:S(2)}, u32[]{:S(2)}) collective-permute-start(bf16[3,96,512]{2,1,0:T(8,128)(2,1)S(1)} %dynamic-slice_bitcast_fusion), channel_id=1, source_target_pairs={{0,16},{16,0},{1,17},{17,1},{2,18},{18,2},{3,19},{19,3},{4,20},{20... | collective-permute-start | bytes 884744 | tf_op jit(solution)/shard_map/ppermute | solution.py:96
  497.4 27.0 %copy-start.24 = (f32[192,1536]{1,0:T(8,128)S(1)}, f32[192,1536]{1,0:T(8,128)}, u32[]{:S(2)}) copy-start(f32[192,1536]{1,0:T(8,128)} %get-tuple-element.39) | copy-start | bytes 3538948
  500.3 6.4 %collective-permute-start.3 = (bf16[96,384]{1,0:T(8,128)(2,1)S(1)}, bf16[96,384]{1,0:T(8,128)(2,1)S(1)}, u32[]{:S(2)}, u32[]{:S(2)}) collective-permute-start(bf16[96,384]{1,0:T(8,128)(2,1)S(1)} %dynamic-slice_bitcast_fusion.1), channel_id=1, source_target_pairs={{0,20},{4,16},{16,4},{20,0},{1,21},{5,17},{17,5},{21,1},{2,22},{6,... | collective-permute-start | bytes 221192 | tf_op jit(solution)/shard_map/ppermute | solution.py:92
  503.3 9.8 %all-to-all-start = ((f32[8,2,96]{2,1,0:T(2,128)}), f32[8,2,96]{2,1,0:T(2,128)S(1)}, u32[]{:S(2)}, u32[]{:S(2)}) async-start(f32[8,2,96]{2,1,0:T(2,128)} %broadcast_in_dim.16), calls=%async_computation.6 | async-start | bytes 16384 | tf_op jit(solution)/shard_map/all_to_all | solution.py:880
  507.9 5.3 collective-permute-start.4
  513.4 4.1 collective-permute-start.5
Sparse Core Ops, SparseCore 0:
  229.7 30.3 reduce-scatter.14
  406.3 62.2 all-reduce.5
  495.7 27.2 reduce-scatter.18
Sparse Core Ops, SparseCore 1:
  246.0 99.8 all-reduce.7
  348.7 20.1 reduce-scatter.20
  371.1 32.8 reduce-scatter.22
  406.4 35.8 reduce-scatter.12
  444.7 50.8 reduce-scatter.16
